TPU v7x, 256 devices: a whole 4x4x8 slice. The times are simulated.
256 devices in a mesh: pop: 16 (over z, y_lo), tp: 16 (over y_hi, x, core).
Axes of the slice: x: 4, y: 4 (y_hi: 2, y_lo: 2; y = y_hi * 2 + y_lo), z: 8, core: 2. Of those that a mesh axis runs over, the one named last changes fastest.
Arguments:
- tokens: bfloat16 [16384, 5120], P('pop', 'tp'), may hold values from -6 to 6
- weight: bfloat16 [5120, 17408], P(None, 'tp'), may hold values from -0.078125 to 0.078125
- factor_a: bfloat16 [128, 4, 5120], P('pop'), may hold values from -6 to 6
- factor_b: bfloat16 [128, 4, 17408], P('pop', None, 'tp'), may hold values from -6 to 6
- member_of_row: int32 [16384], P('pop'), may hold values from 0 to 127, as said below
- fitness_rank: int32 [128], P('pop'), may hold values from 0 to 127, each once
Outputs:
- activations: bfloat16 [16384, 17408], P('pop', 'tp')
- update: bfloat16 [5120, 17408], P('pop', 'tp')
Inputs may be any that keep to these rules, and one draw needn't show every extreme that they name: `member_of_row`: the rows held by index p of pop belong to members p * 8 to (p + 1) * 8 - 1, each member owning exactly 128 of them, in a random order. `fitness_rank`: A permutation of the members' ranks.
All inputs are finite; a program needn't handle non-finite values.
Results may differ from a plain program's by a relative error of at most 0.0049.
Values may be sent and summed in bfloat16 or wider, within the bound.
No kernel may reach another device: no remote copies, remote signals or barrier semaphores. Data moves between devices by JAX's collectives and lax.ppermute only.
A program may use at most 128 MiB of HBM per device.

v0:
```python
import math

import jax
import jax.numpy as jnp
from jax import lax
from jax.sharding import PartitionSpec as P

perturb_scale = 0.5


def contract_rows(left, right):
    return lax.dot_general(
        left, right, (((0,), (0,)), ((), ())), preferred_element_type=jnp.float32
    )


def contract_cols(left, right):
    return lax.dot_general(
        left, right, (((1,), (1,)), ((), ())), preferred_element_type=jnp.float32
    )


def body(tokens, weight, factor_a, factor_b, member_of_row, fitness_rank):
    members, factor_rank, model_width = factor_a.shape
    hidden_cols = weight.shape[1]
    token_rows = tokens.shape[0]
    pop_index = lax.axis_index("pop")
    flat_a = factor_a.reshape(members * factor_rank, model_width)
    flat_b = factor_b.reshape(members * factor_rank, hidden_cols)
    segment = lax.all_gather(tokens, "tp", axis=1, tiled=True)
    preact = jnp.dot(segment, weight, preferred_element_type=jnp.float32)
    lowrank = contract_cols(segment, flat_a)
    local_member = member_of_row - pop_index * members
    onehot = (local_member[:, None] == jnp.arange(members, dtype=jnp.int32)[None, :]).astype(
        jnp.float32
    )
    coefficient = (
        lowrank.reshape(token_rows, members, factor_rank)
        * onehot[:, :, None]
        * (perturb_scale / math.sqrt(model_width))
    )
    coefficient = coefficient.reshape(token_rows, members * factor_rank).astype(jnp.bfloat16)
    correction = jnp.dot(coefficient, flat_b, preferred_element_type=jnp.float32)
    activations = jax.nn.silu(preact + correction).astype(jnp.bfloat16)
    population = members * lax.axis_size("pop")
    fitness = 2.0 * fitness_rank.astype(jnp.float32) / (population - 1) - 1.0
    scaled_b = (factor_b.astype(jnp.float32) * fitness[:, None, None]).astype(jnp.bfloat16)
    own_rows = model_width // lax.axis_size("pop")
    a_rows = lax.dynamic_slice_in_dim(
        lax.all_gather(factor_a, "pop", axis=0, tiled=True), pop_index * own_rows, own_rows, 2
    )
    summed = contract_rows(
        a_rows.reshape(-1, own_rows),
        lax.all_gather(scaled_b, "pop", axis=0, tiled=True).reshape(-1, hidden_cols),
    )
    update = (summed * (1.0 / math.sqrt(population * factor_rank))).astype(jnp.bfloat16)
    return (activations, update)


def solution(mesh):
    placed = (
        P("pop", "tp"),
        P(None, "tp"),
        P("pop", None, None),
        P("pop", None, "tp"),
        P("pop"),
        P("pop"),
    )
    return jax.shard_map(
        body,
        mesh=mesh,
        in_specs=placed,
        out_specs=(P("pop", "tp"), P("pop", "tp")),
        check_vma=False,
    )
```

profile of v0, /device:TPU:1, one launch (start us, length us, event | category | flops | bytes accessed | tf_op | source)
XLA Modules:
  0.0 330.3 jit_solution(5377419649255138807)
XLA Ops:
  7.2 0.0 copy-start
  7.2 0.0 copy-start.1
  7.2 0.0 all-gather.6.cloned.1.call-start
  7.2 0.7 all-gather.6.cloned.1.call-update
  7.9 0.0 all-gather.8.cloned.1.call-start
  8.0 0.7 multiply_add_fusion
  8.6 1.6 multiply_convert_fusion.1
  10.2 0.0 all-gather.8.cloned.1.call-update
  10.2 0.0 all-gather.4.cloned.1.call-start
  10.3 0.7 all-gather.4.cloned.1.call-update
  11.0 0.7 broadcast_subtract_fusion
  11.7 120.7 %all-gather.6.cloned.1.call-done = bf16[128,4,5120]{2,1,0:T(4,128)(2,1)} async-done(((bf16[8,4,5120]{2,1,0:T(4,128)(2,1)}), bf16[128,4,5120]{2,1,0:T(4,128)(2,1)}) %all-gather.6.cloned.1.call-update) | async-done | bytes 5242896 | tf_op jit(solution)/shard_map/all_gather | solution.py:50
  132.4 1.3 constant_dynamic-slice_fusion
  133.7 61.8 %all-gather.8.cloned.1.call-done = bf16[128,4,1088]{2,0,1:T(8,128)(2,1)} async-done(((bf16[8,4,1088]{2,0,1:T(8,128)(2,1)}), bf16[128,4,1088]{2,0,1:T(8,128)(2,1)}) %all-gather.8.cloned.1.call-update) | async-done | bytes 1114128 | tf_op jit(solution)/shard_map/all_gather | solution.py:54
  195.5 2.8 fusion.3
  198.3 97.7 %all-gather.4.cloned.1.call-done = bf16[1024,5120]{0,1:T(8,128)(2,1)} async-done(((bf16[1024,320]{0,1:T(8,128)(2,1)}), bf16[1024,5120]{0,1:T(8,128)(2,1)}) %all-gather.4.cloned.1.call-update) | async-done | bytes 10485776 | tf_op jit(solution)/shard_map/all_gather | solution.py:30
  296.0 0.0 copy-done
  296.0 0.0 copy-done.1
  296.0 8.6 %fusion.14 = f32[1024,1088,1]{0,1,2:T(8,128)} fusion(bf16[1024,5120]{0,1:T(8,128)(2,1)} %all-gather.4.cloned.1.call-done, bf16[8,4,5120]{2,1,0:T(4,128)(2,1)S(1)} %copy-done, f32[1024,8]{0,1:T(8,128)S(1)} %fusion.22, bf16[8,4,1088]{2,1,0:T(4,128)(2,1)S(1)} %copy-done.1), kind=kOutput, calls=%fused_computation.10 | convolution fusion | flops 406945792 | bytes 15372288 | tf_op jit(solution)/shard_map/dot_general | solution.py:43
  304.6 19.2 %multiply_convert_fusion = bf16[1024,1088]{0,1:T(8,128)(2,1)} fusion(f32[1024,1088,1]{0,1,2:T(8,128)} %fusion.14, bf16[5120,1088]{0,1:T(8,128)(2,1)} %param.7, bf16[1024,5120]{0,1:T(8,128)(2,1)} %all-gather.4.cloned.1.call-done), kind=kOutput, calls=%fused_computation.3 | convolution fusion | flops 11415191552 | bytes 28311552 | tf_op jit(solution)/shard_map/dot_general | solution.py:31
  (1 shorter events, 0.0 us)
Async XLA Ops:
  7.2 288.8 %copy-start = (bf16[8,4,5120]{2,1,0:T(4,128)(2,1)S(1)}, bf16[8,4,5120]{2,1,0:T(4,128)(2,1)}, u32[]{:S(2)}) copy-start(bf16[8,4,5120]{2,1,0:T(4,128)(2,1)} %param.8) | copy-start | bytes 983044
  7.2 288.8 %copy-start.1 = (bf16[8,4,1088]{2,1,0:T(4,128)(2,1)S(1)}, bf16[8,4,1088]{2,1,0:T(4,128)(2,1)}, u32[]{:S(2)}) copy-start(bf16[8,4,1088]{2,1,0:T(4,128)(2,1)} %param.9) | copy-start | bytes 208900
  7.2 125.2 %all-gather.6.cloned.1.call-start = ((), (), s32[]{:S(2)}) async-start(), calls=%async_computation.1 | async-start | bytes 5570560 | tf_op jit(solution)/shard_map/all_gather | solution.py:50
  7.9 187.6 %all-gather.8.cloned.1.call-start = ((), (), s32[]{:S(2)}) async-start(), calls=%async_computation.2 | async-start | bytes 1253376 | tf_op jit(solution)/shard_map/all_gather | solution.py:54
  10.2 285.7 %all-gather.4.cloned.1.call-start = ((), (), s32[]{:S(2)}) async-start(), calls=%async_computation | async-start | bytes 11141120 | tf_op jit(solution)/shard_map/all_gather | solution.py:30
Sparse Core Ops, SparseCore 0:
  9.8 122.5 all-gather.5
  134.8 60.7 all-gather.7
  198.3 97.6 all-gather.3
where the time goes:
time: 331 us; the launch traced here: 330 us
  waiting for transfers between devices  282 us (85%)
  matrix products  30.5 us (9%)
  between operations  13.8 us (4%)
    all_gather x1, waiting for transfers between devices, body(): lax.all_gather(factor_a, 'pop', axis=0, tiled=True)  121 us
    all_gather x1, waiting for transfers between devices, body(): segment = lax.all_gather(tokens, 'tp', axis=1, tiled=True)  97.7 us
    all_gather x1, waiting for transfers between devices, body(): lax.all_gather(scaled_b, 'pop', axis=0, tiled=True).reshape(-1, hidden_cols)  61.8 us
    dot_general x1, matrix products, body(): preact = jnp.dot(segment, weight, preferred_element_type=jnp.float32)  19.2 us
    dot_general x1, matrix products, body(): jnp.dot(coefficient, flat_b, preferred_element_type=jnp.float32)  8.63 us
  transfers between devices with their start and end apart: 3, of which 3 were waited for; matrix products, arithmetic and copies ran while one was open for 2% of the time, Pallas kernels for 0%

commit v1 on v0

v1 whole, which is shorter than its diff:
```python
import functools
import math

import jax
import jax.numpy as jnp
from jax import lax
from jax.experimental import pallas as pl
from jax.experimental.pallas import tpu as pltpu
from jax.sharding import PartitionSpec as P

perturb_scale = 0.5
f32, bf16 = jnp.float32, jnp.bfloat16

D, COLS, ROWS, SHARD = 5120, 1088, 1024, 320
CHIP = 2 * SHARD
LOW = 32
TALL = COLS + LOW
NB = 256
WIDE = 384
PAY = WIDE + COLS
POPS, XS = 16, 4
VMEM = 56 * 2**20

TP = [(y, x, c) for y in range(2) for x in range(XS) for c in range(2)]


def tp_at(y, x, c):
    return ((y % 2) * XS + x % XS) * 2 + c % 2


X_UP = [(tp_at(y, x, c), tp_at(y, x + 1, c)) for y, x, c in TP]
X_DOWN = [(tp_at(y, x, c), tp_at(y, x - 1, c)) for y, x, c in TP]
Y_SWAP = [(tp_at(y, x, c), tp_at(y + 1, x, c)) for y, x, c in TP]
CORE_SWAP = [(tp_at(y, x, c), tp_at(y, x, c + 1)) for y, x, c in TP]


def cost(flops, nbytes):
    return pl.CostEstimate(flops=int(flops), bytes_accessed=int(nbytes), transcendentals=0)


def load_group(chips, pieces, s, w, a, mine, other, wx, xs, sem):
    copies = []
    for k in range(chips):
        col = pl.multiple_of(s[k] * CHIP, 128)
        copies.append((w.at[:, pl.ds(col, CHIP)], wx.at[pl.ds(0, COLS), pl.ds(k * CHIP, CHIP)]))
        copies.append((a.at[:, pl.ds(col, CHIP)], wx.at[pl.ds(COLS, LOW), pl.ds(k * CHIP, CHIP)]))
    core = s[chips]
    start = 0
    for piece, (m, o) in enumerate(zip(mine, other)):
        chip, within = pieces[piece]
        size = m.shape[0]
        base = chip * CHIP + within
        m_row = pl.multiple_of(base + core * SHARD, 16)
        o_row = pl.multiple_of(base + (1 - core) * SHARD, 16)
        copies.append((m, xs.at[pl.ds(m_row, size), :]))
        copies.append((o, xs.at[pl.ds(o_row, size), :]))
    handles = [pltpu.make_async_copy(src, dst, sem.at[i]) for i, (src, dst) in enumerate(copies)]
    for h in handles:
        h.start()
    for h in handles:
        h.wait()


def group_kernel(chips, pieces, first, last, s, *refs):
    n = len(pieces)
    w, a = refs[0], refs[1]
    mine, other = refs[2 : 2 + n], refs[2 + n : 2 + 2 * n]
    rest = list(refs[2 + 2 * n :])
    acc = None if first else rest.pop(0)
    if last:
        b, member = rest.pop(0), rest.pop(0)
    out, wx, xs, sem = rest
    j = pl.program_id(0)

    @pl.when(j == 0)
    def _():
        load_group(chips, pieces, s, w, a, mine, other, wx, xs, sem)

    cols = pl.ds(pl.multiple_of(j * NB, NB), NB)
    part = jnp.dot(wx[...], xs[:, cols], preferred_element_type=f32)
    if not first:
        part = part + acc[...]
    if not last:
        out[...] = part
        return
    low = part[COLS:, :] * (perturb_scale / math.sqrt(D))
    rank_row = lax.broadcasted_iota(jnp.int32, (LOW, NB), 0) >> 2
    local = member[...] - s[chips + 1] * 8
    coef = jnp.where(rank_row == local, low, 0.0).astype(bf16)
    corr = lax.dot_general(b[...], coef, (((0,), (0,)), ((), ())), preferred_element_type=f32)
    v = part[:COLS, :] + corr
    out[...] = (v * (1.0 / (1.0 + jnp.exp(-v)))).astype(bf16)


def group(chips, pieces, scalars, w, a, mine, other, acc=None, last=None):
    n = len(pieces)
    any_spec = pl.BlockSpec(memory_space=pl.ANY)
    column = pl.BlockSpec((TALL, NB), lambda j, s: (0, j))
    in_specs = [any_spec] * (2 + 2 * n)
    args = [w, a, *mine, *other]
    if acc is not None:
        in_specs.append(column)
        args.append(acc)
    if last is not None:
        in_specs += [
            pl.BlockSpec((LOW, COLS), lambda j, s: (0, 0)),
            pl.BlockSpec((1, NB), lambda j, s: (0, j)),
        ]
        args += list(last)
        out_shape = jax.ShapeDtypeStruct((COLS, ROWS), bf16)
        out_spec = pl.BlockSpec((COLS, NB), lambda j, s: (0, j))
    else:
        out_shape = jax.ShapeDtypeStruct((TALL, ROWS), f32)
        out_spec = column
    depth = chips * CHIP
    return pl.pallas_call(
        functools.partial(group_kernel, chips, pieces, acc is None, last is not None),
        out_shape=out_shape,
        grid_spec=pltpu.PrefetchScalarGridSpec(
            num_scalar_prefetch=1,
            grid=(ROWS // NB,),
            in_specs=in_specs,
            out_specs=out_spec,
            scratch_shapes=[
                pltpu.VMEM((TALL, depth), bf16),
                pltpu.VMEM((depth, ROWS), bf16),
                pltpu.SemaphoreType.DMA((2 * chips + 2 * n,)),
            ],
        ),
        compiler_params=pltpu.CompilerParams(vmem_limit_bytes=VMEM),
        cost_estimate=cost(2 * TALL * depth * ROWS, 2 * depth * (TALL + ROWS) + 8 * TALL * ROWS),
    )(scalars, *args)


def payload_kernel(a, b, fit, out):
    scaled = (b[...].astype(f32) * fit[...]).astype(bf16)
    for p in range(POPS):
        start = (p * SHARD) // 128 * 128
        out[p, :, :WIDE] = a[:, start : start + WIDE]
        out[p, :, WIDE:] = scaled


def update_kernel(s, got, out, wide):
    wide[...] = lax.dot_general(
        got[:, :WIDE], got[:, WIDE:], (((0,), (0,)), ((), ())), preferred_element_type=f32
    )
    first = pl.multiple_of(s[0] * 64, 64)
    out[...] = (wide[pl.ds(first, SHARD), :] * (1.0 / math.sqrt(512))).astype(bf16)


def body(tokens, weight, factor_a, factor_b, member_of_row, fitness_rank):
    pop = lax.axis_index("pop")
    tp = lax.axis_index("tp")
    core, x, y = tp % 2, (tp // 2) % XS, tp // (2 * XS)
    shard = tokens.T
    w = weight.T
    a = factor_a.reshape(LOW, D)
    b = factor_b.reshape(LOW, COLS)

    send = lambda v, perm: lax.ppermute(v, "tp", perm)
    swap = lambda v: send(v, CORE_SWAP)

    low_x = send(shard, X_UP)
    high_x = send(shard, X_DOWN)
    far_y = send(shard, Y_SWAP)
    own_o = swap(shard)

    fitness = 2.0 * fitness_rank.astype(f32) / 127.0 - 1.0
    payload = pl.pallas_call(
        payload_kernel,
        out_shape=jax.ShapeDtypeStruct((POPS, LOW, PAY), bf16),
        compiler_params=pltpu.CompilerParams(vmem_limit_bytes=VMEM),
        cost_estimate=cost(LOW * COLS, POPS * LOW * PAY * 2),
    )(a, b, jnp.repeat(fitness, 4)[:, None])
    got = lax.all_to_all(payload, "pop", 0, 0, tiled=True)

    two_x = send(low_x, X_UP)
    far_high = send(far_y, X_DOWN)
    far_low = send(low_x, Y_SWAP)
    o1 = [own_o, swap(low_x), swap(high_x), swap(far_y)]

    e = [send(far_low[:112], X_UP), send(two_x[112:208], Y_SWAP), send(far_high[208:], X_DOWN)]
    o2 = [swap(two_x), swap(far_high), swap(far_low)]
    oe = [swap(v) for v in e]

    chip = lambda dy, dx: ((y + dy) % 2) * XS + (x + dx) % XS
    ints = lambda *v: jnp.stack([jnp.asarray(i, jnp.int32) for i in v])
    acc = group(
        4,
        ((0, 0), (1, 0), (2, 0), (3, 0)),
        ints(chip(0, 0), chip(0, -1), chip(0, 1), chip(1, 0), core),
        w,
        a,
        [shard, low_x, high_x, far_y],
        o1,
    )
    update = pl.pallas_call(
        update_kernel,
        out_shape=jax.ShapeDtypeStruct((SHARD, COLS), bf16),
        grid_spec=pltpu.PrefetchScalarGridSpec(
            num_scalar_prefetch=1,
            grid=(1,),
            in_specs=[pl.BlockSpec((POPS * LOW, PAY), lambda j, s: (0, 0))],
            out_specs=pl.BlockSpec((SHARD, COLS), lambda j, s: (0, 0)),
            scratch_shapes=[pltpu.VMEM((WIDE, COLS), f32)],
        ),
        compiler_params=pltpu.CompilerParams(vmem_limit_bytes=VMEM),
        cost_estimate=cost(2 * 512 * WIDE * COLS, 512 * PAY * 2 + SHARD * COLS * 2),
    )(ints(pop % 2), got.reshape(POPS * LOW, PAY))
    acc = group(
        3,
        ((0, 0), (1, 0), (2, 0)),
        ints(chip(0, 2), chip(1, 1), chip(1, -1), core),
        w,
        a,
        [two_x, far_high, far_low],
        o2,
        acc=acc,
    )
    act = group(
        1,
        ((0, 0), (0, 112), (0, 208)),
        ints(chip(1, 2), core, pop),
        w,
        a,
        e,
        oe,
        acc=acc,
        last=(b, member_of_row.reshape(1, ROWS)),
    )
    return (act.T, update)


def solution(mesh):
    placed = (
        P("pop", "tp"),
        P(None, "tp"),
        P("pop", None, None),
        P("pop", None, "tp"),
        P("pop"),
        P("pop"),
    )
    return jax.shard_map(
        body,
        mesh=mesh,
        in_specs=placed,
        out_specs=(P("pop", "tp"), P("pop", "tp")),
        check_vma=False,
    )
```

time: 331 us -> 120 us (0.36)
  waiting for transfers between devices: 282 us -> 37.3 us
  Pallas kernels: 0 us -> 40.6 us
  matrix products: 30.5 us -> 0 us
  starting transfers between devices: 0.12 us -> 30.5 us
  between operations: 13.8 us -> 0.87 us
  local copies, waits for them, and re-layouts: 1.35 us -> 8.4 us
    all_gather x3 -> x0, waiting for transfers between devices: 280 us -> none  [the longest x1 121 us: body(): lax.all_gather(factor_a, 'pop', axis=0, tiled=True)]
    pallas_call x0 -> x5, Pallas kernels: none -> 40.6 us  [the longest x3 35.1 us: group(): pl.pallas_call(functools.partial(group_kernel, chips, pieces, acc is None...]
    ppermute x0 -> x19, waiting for transfers between devices: none -> 37.3 us  [body(): send = lambda v, perm: lax.ppermute(v, 'tp', perm)]
    dot_general x3 -> x0, matrix products: 30.5 us -> none  [the longest x1 19.2 us: body(): preact = jnp.dot(segment, weight, preferred_element_type=jnp.float32)]
    ppermute x0 -> x19, starting transfers between devices: none -> 21.2 us  [body(): send = lambda v, perm: lax.ppermute(v, 'tp', perm)]
    all_to_all x0 -> x1, starting transfers between devices: none -> 9.3 us  [body(): got = lax.all_to_all(payload, 'pop', 0, 0, tiled=True)]
    unnamed x4 -> x30, local copies, waits for them, and re-layouts: 0.01 us -> 3.66 us
    reshape x0 -> x2, local copies, waits for them, and re-layouts: none -> 3.32 us  [the longest x1 1.77 us: body(): a = factor_a.reshape(LOW, D)]
  transfers between devices with their start and end apart: 3 -> 20, of which waited for: 3 -> 3; matrix products, arithmetic and copies ran while one was open for 2% -> 6% of each run, Pallas kernels for 0% -> 31%
where the time goes in v1:
time: 120 us; the launch traced here: 119 us
  Pallas kernels  40.6 us (34%)
  waiting for transfers between devices  37.3 us (31%)
  starting transfers between devices  30.5 us (25%)
  local copies, waits for them, and re-layouts  8.4 us (7%)
  other arithmetic  1.89 us (2%)
    ppermute x19, waiting for transfers between devices, body(): send = lambda v, perm: lax.ppermute(v, 'tp', perm)  37.3 us
    pallas_call x3, Pallas kernels, group(): pl.pallas_call(functools.partial(group_kernel, chips, pieces, acc is None...  35.1 us
    ppermute x19, starting transfers between devices, body(): send = lambda v, perm: lax.ppermute(v, 'tp', perm)  21.2 us
    all_to_all x1, starting transfers between devices, body(): got = lax.all_to_all(payload, 'pop', 0, 0, tiled=True)  9.3 us
    unnamed x30, local copies, waits for them, and re-layouts  3.66 us
    pallas_call x1, Pallas kernels, body(): pl.pallas_call(update_kernel, out_shape=jax.ShapeDtypeStruct((SHARD, COLS...  3.13 us
  transfers between devices with their start and end apart: 20, of which 3 were waited for; matrix products, arithmetic and copies ran while one was open for 6% of the time, Pallas kernels for 31%

profile of v1, /device:TPU:1, one launch (start us, length us, event | category | flops | bytes accessed | tf_op | source)
XLA Modules:
  0.0 119.5 jit_solution(13909020057264705849)
XLA Ops:
  0.6 0.0 copy-start.13
  0.6 2.1 %collective-permute-start = (bf16[320,1024]{1,0:T(8,128)(2,1)}, bf16[320,1024]{1,0:T(8,128)(2,1)}, u32[]{:S(2)}, u32[]{:S(2)}) collective-permute-start(bf16[320,1024]{1,0:T(8,128)(2,1)} %bitcast.22), channel_id=1, source_target_pairs={{0,2},{1,3},{2,4},{3,5},{4,6},{5,7},{6,0},{7,1},{8,10},{9,11},{10,... | collective-permute-start | bytes 1966088 | tf_op jit(solution)/shard_map/ppermute | solution.py:160
  2.8 1.8 %reshape.16.refs_1_.a = bf16[32,5120]{1,0:T(8,128)(2,1)} reshape(bf16[8,4,5120]{2,1,0:T(4,128)(2,1)} %param.8) | data formatting | bytes 655360 | tf_op jit(solution)/shard_map/reshape | solution.py:157
  4.5 1.5 %reshape.17.refs_9_.b = bf16[32,1088]{1,0:T(8,128)(2,1)} reshape(bf16[8,4,1088]{2,1,0:T(4,128)(2,1)} %param.9) | data formatting | bytes 139264 | tf_op jit(solution)/shard_map/reshape | solution.py:158
  6.1 0.7 multiply_add_fusion
  6.7 0.1 broadcast_in_dim.3
  6.8 0.7 broadcast_in_dim_reshape.4.fit
  7.5 2.3 %shard_map.80 = bf16[16,32,1472]{2,1,0:T(8,128)(2,1)} custom-call(bf16[32,5120]{1,0:T(8,128)(2,1)} %reshape.16.refs_1_.a, bf16[32,1088]{1,0:T(8,128)(2,1)} %reshape.17.refs_9_.b, f32[32,1]{1,0:T(8,128)} %broadcast_in_dim_reshape.4.fit), custom_call_target="tpu_custom_call" | custom-call | flops 34816 | bytes 1507328 | tf_op jit(solution)/shard_map/pallas_call | solution.py:169
  9.8 9.3 %all-to-all-start = ((bf16[16,32,1472]{2,1,0:T(8,128)(2,1)}), bf16[16,32,1472]{2,1,0:T(8,128)(2,1)S(1)}, u32[]{:S(2)}, u32[]{:S(2)}) async-start(bf16[16,32,1472]{2,1,0:T(8,128)(2,1)} %shard_map.80), calls=%async_computation | async-start | bytes 3145728 | tf_op jit(solution)/shard_map/all_to_all | solution.py:175
  19.1 2.7 %collective-permute-start.5 = (bf16[320,1024]{1,0:T(8,128)(2,1)S(1)}, bf16[320,1024]{1,0:T(8,128)(2,1)}, u32[]{:S(2)}, u32[]{:S(2)}) collective-permute-start(bf16[320,1024]{1,0:T(8,128)(2,1)S(1)} %bitcast.24), channel_id=1, source_target_pairs={{0,8},{1,9},{2,10},{3,11},{4,12},{5,13},{6,14},{7,15},{8,0},{9,1},... | collective-permute-start | bytes 1966088 | tf_op jit(solution)/shard_map/ppermute | solution.py:160
  21.8 1.5 %collective-permute-start.14 = (bf16[320,1024]{1,0:T(8,128)(2,1)S(1)}, bf16[320,1024]{1,0:T(8,128)(2,1)}, u32[]{:S(2)}, u32[]{:S(2)}) collective-permute-start(bf16[320,1024]{1,0:T(8,128)(2,1)S(1)} %bitcast.25), channel_id=1, source_target_pairs={{0,6},{1,7},{2,0},{3,1},{4,2},{5,3},{6,4},{7,5},{8,14},{9,15},{10,... | collective-permute-start | bytes 1966088 | tf_op jit(solution)/shard_map/ppermute | solution.py:160
  23.3 1.8 %collective-permute-start.15 = (bf16[320,1024]{1,0:T(8,128)(2,1)S(1)}, bf16[320,1024]{1,0:T(8,128)(2,1)S(1)}, u32[]{:S(2)}, u32[]{:S(2)}) collective-permute-start(bf16[320,1024]{1,0:T(8,128)(2,1)S(1)} %bitcast.26), channel_id=1, source_target_pairs={{0,1},{1,0},{2,3},{3,2},{4,5},{5,4},{6,7},{7,6},{8,9},{9,8},{10,11... | collective-permute-start | bytes 1966088 | tf_op jit(solution)/shard_map/ppermute | solution.py:160
  25.1 0.0 collective-permute-done.refs_3_
  25.1 0.0 collective-permute-start.3
  25.1 0.3 collective-permute-start.16
  25.4 13.5 %collective-permute-done.5.refs_5_ = bf16[320,1024]{1,0:T(8,128)(2,1)} collective-permute-done((bf16[320,1024]{1,0:T(8,128)(2,1)S(1)}, bf16[320,1024]{1,0:T(8,128)(2,1)}, u32[]{:S(2)}, u32[]{:S(2)}) %collective-permute-start.5) | collective-permute-done | bytes 655392 | tf_op jit(solution)/shard_map/ppermute | solution.py:160
  38.9 2.1 %collective-permute-start.18 = (bf16[320,1024]{1,0:T(8,128)(2,1)}, bf16[320,1024]{1,0:T(8,128)(2,1)}, u32[]{:S(2)}, u32[]{:S(2)}) collective-permute-start(bf16[320,1024]{1,0:T(8,128)(2,1)} %collective-permute-done.5.refs_5_), channel_id=1, source_target_pairs={{0,1},{1,0},{2,3},{3,2},{4,5},{5,4},{6,7},{7,6},{8,9},{9,8},{10,11... | collective-permute-start | bytes 1966088 | tf_op jit(solution)/shard_map/ppermute | solution.py:160
  41.1 0.0 collective-permute-done.14.refs_4_
  41.1 1.0 collective-permute-start.1
  42.0 1.5 %collective-permute-start.6 = (bf16[320,1024]{1,0:T(8,128)(2,1)}, bf16[320,1024]{1,0:T(8,128)(2,1)S(1)}, u32[]{:S(2)}, u32[]{:S(2)}) collective-permute-start(bf16[320,1024]{1,0:T(8,128)(2,1)} %collective-permute-done.5.refs_5_), channel_id=1, source_target_pairs={{0,6},{1,7},{2,0},{3,1},{4,2},{5,3},{6,4},{7,5},{8,14},{9,15},{10,... | collective-permute-start | bytes 1966088 | tf_op jit(solution)/shard_map/ppermute | solution.py:160
  43.5 0.6 collective-permute-start.17
  44.1 0.6 stack.56.s
  44.8 2.1 %collective-permute-start.4 = (bf16[96,1024]{1,0:T(8,128)(2,1)S(1)}, bf16[96,1024]{1,0:T(8,128)(2,1)S(1)}, u32[]{:S(2)}, u32[]{:S(2)}) collective-permute-start(bf16[96,1024]{1,0:T(8,128)(2,1)S(1)} %slice.13), channel_id=1, source_target_pairs={{0,8},{1,9},{2,10},{3,11},{4,12},{5,13},{6,14},{7,15},{8,0},{9,1},... | collective-permute-start | bytes 589832 | tf_op jit(solution)/shard_map/ppermute | solution.py:160
  46.9 0.6 pad_add_fusion.s
  47.5 0.0 collective-permute-done.18.refs_9_
  47.5 0.4 collective-permute-start.11
  48.0 22.3 %collective-permute-done.1.refs_4_ = bf16[320,1024]{1,0:T(8,128)(2,1)S(1)} collective-permute-done((bf16[320,1024]{1,0:T(8,128)(2,1)}, bf16[320,1024]{1,0:T(8,128)(2,1)S(1)}, u32[]{:S(2)}, u32[]{:S(2)}) %collective-permute-start.1) | collective-permute-done | bytes 655392 | tf_op jit(solution)/shard_map/ppermute | solution.py:160
  70.3 0.8 collective-permute-start.13
  71.0 0.1 collective-permute-start.12
  71.2 0.6 pad_add_fusion.1.s
  71.8 1.3 %collective-permute-start.2 = (bf16[112,1024]{1,0:T(8,128)(2,1)S(1)}, bf16[112,1024]{1,0:T(8,128)(2,1)S(1)}, u32[]{:S(2)}, u32[]{:S(2)}) collective-permute-start(bf16[112,1024]{1,0:T(8,128)(2,1)S(1)} %slice.12), channel_id=1, source_target_pairs={{0,2},{1,3},{2,4},{3,5},{4,6},{5,7},{6,0},{7,1},{8,10},{9,11},{10,... | collective-permute-start | bytes 688136 | tf_op jit(solution)/shard_map/ppermute | solution.py:160
  73.1 1.4 %collective-permute-done.4.refs_3_ = bf16[96,1024]{1,0:T(8,128)(2,1)S(1)} collective-permute-done((bf16[96,1024]{1,0:T(8,128)(2,1)S(1)}, bf16[96,1024]{1,0:T(8,128)(2,1)S(1)}, u32[]{:S(2)}, u32[]{:S(2)}) %collective-permute-start.4) | collective-permute-done | bytes 196640 | tf_op jit(solution)/shard_map/ppermute | solution.py:160
  74.5 1.5 %collective-permute-start.7 = (bf16[112,1024]{1,0:T(8,128)(2,1)S(1)}, bf16[112,1024]{1,0:T(8,128)(2,1)S(1)}, u32[]{:S(2)}, u32[]{:S(2)}) collective-permute-start(bf16[112,1024]{1,0:T(8,128)(2,1)S(1)} %slice.14), channel_id=1, source_target_pairs={{0,6},{1,7},{2,0},{3,1},{4,2},{5,3},{6,4},{7,5},{8,14},{9,15},{10,... | collective-permute-start | bytes 688136 | tf_op jit(solution)/shard_map/ppermute | solution.py:160
  76.0 12.9 %shard_map.77.refs_8_ = f32[1120,1024]{1,0:T(8,128)} custom-call(s32[5]{0:T(128)} %stack.56.s, bf16[1088,5120]{1,0:T(8,128)(2,1)} %bitcast.16, bf16[32,5120]{1,0:T(8,128)(2,1)} %reshape.16.refs_1_.a, bf16[320,1024]{1,0:T(8,128)(2,1)} %bitcast.23, bf16[320,1024]{1,0:T(8,128)(2,1)} %collective-permute-done.refs_3_, ...), custom_call_target="tpu_custom_call" | custom-call | flops 5872025600 | bytes 20152320 | tf_op jit(solution)/shard_map/pallas_call | solution.py:116
  88.9 0.9 collective-permute-start.9
  89.9 0.1 collective-permute-start.8
  90.0 0.4 collective-permute-start.10
  90.4 0.4 copy-done.4
  90.8 0.4 copy-done.5
  91.2 0.9 copy-done.6
  92.1 12.5 %shard_map.78.refs_8_ = f32[1120,1024]{1,0:T(8,128)} custom-call(s32[4]{0:T(128)} %pad_add_fusion.1.s, bf16[1088,5120]{1,0:T(8,128)(2,1)} %bitcast.17, bf16[32,5120]{1,0:T(8,128)(2,1)} %reshape.16.refs_1_.a, bf16[320,1024]{1,0:T(8,128)(2,1)} %copy-done.3, bf16[320,1024]{1,0:T(8,128)(2,1)} %copy-done.2, bf16[320,1024]{1,0:T(8,128)(2,1)} %copy-done.1, ...), custom_call_target="tpu_custom_call" | custom-call | flops 4404019200 | bytes 17408000 | tf_op jit(solution)/shard_map/pallas_call | solution.py:116
  104.6 0.0 copy-start.9
  104.7 0.6 copy-done.12
  105.3 0.1 copy-done.9
  105.3 0.1 copy-done.10
  105.4 9.8 %shard_map.79 = bf16[1088,1024]{1,0:T(8,128)(2,1)} custom-call(s32[3]{0:T(128)} %pad_add_fusion.s, bf16[1088,5120]{1,0:T(8,128)(2,1)} %bitcast.18, bf16[32,5120]{1,0:T(8,128)(2,1)} %reshape.16.refs_1_.a, bf16[112,1024]{1,0:T(8,128)(2,1)} %copy-done.7, bf16[96,1024]{1,0:T(8,128)(2,1)} %copy-done.11, bf16[112,1024]{1,0:T(8,128)(2,1)} %copy-done.8, ...), custom_call_target="tpu_custom_call" | custom-call | flops 1468006400 | bytes 11919360 | tf_op jit(solution)/shard_map/pallas_call | solution.py:116
  115.2 1.2 copy-done
  116.4 3.1 %shard_map.81 = bf16[320,1088]{1,0:T(8,128)(2,1)} custom-call(s32[1]{0:T(128)} %bitcast.14.s, bf16[512,1472]{1,0:T(8,128)(2,1)} %bitcast.19), custom_call_target="tpu_custom_call" | custom-call | flops 427819008 | bytes 2203648 | tf_op jit(solution)/shard_map/pallas_call | solution.py:197
  (38 shorter events, 0.1 us)
Async XLA Ops:
  0.6 18.5 %copy-start.13 = (bf16[1024,320]{0,1:T(8,128)(2,1)S(1)}, bf16[1024,320]{0,1:T(8,128)(2,1)}, u32[]{:S(2)}) copy-start(bf16[1024,320]{0,1:T(8,128)(2,1)} %param.6) | copy-start | bytes 1966084
  0.6 24.5 %collective-permute-start = (bf16[320,1024]{1,0:T(8,128)(2,1)}, bf16[320,1024]{1,0:T(8,128)(2,1)}, u32[]{:S(2)}, u32[]{:S(2)}) collective-permute-start(bf16[320,1024]{1,0:T(8,128)(2,1)} %bitcast.22), channel_id=1, source_target_pairs={{0,2},{1,3},{2,4},{3,5},{4,6},{5,7},{6,0},{7,1},{8,10},{9,11},{10,... | collective-permute-start | bytes 1966088 | tf_op jit(solution)/shard_map/ppermute | solution.py:160
  9.8 105.4 %all-to-all-start = ((bf16[16,32,1472]{2,1,0:T(8,128)(2,1)}), bf16[16,32,1472]{2,1,0:T(8,128)(2,1)S(1)}, u32[]{:S(2)}, u32[]{:S(2)}) async-start(bf16[16,32,1472]{2,1,0:T(8,128)(2,1)} %shard_map.80), calls=%async_computation | async-start | bytes 3145728 | tf_op jit(solution)/shard_map/all_to_all | solution.py:175
  19.1 19.8 %collective-permute-start.5 = (bf16[320,1024]{1,0:T(8,128)(2,1)S(1)}, bf16[320,1024]{1,0:T(8,128)(2,1)}, u32[]{:S(2)}, u32[]{:S(2)}) collective-permute-start(bf16[320,1024]{1,0:T(8,128)(2,1)S(1)} %bitcast.24), channel_id=1, source_target_pairs={{0,8},{1,9},{2,10},{3,11},{4,12},{5,13},{6,14},{7,15},{8,0},{9,1},... | collective-permute-start | bytes 1966088 | tf_op jit(solution)/shard_map/ppermute | solution.py:160
  21.8 19.2 %collective-permute-start.14 = (bf16[320,1024]{1,0:T(8,128)(2,1)S(1)}, bf16[320,1024]{1,0:T(8,128)(2,1)}, u32[]{:S(2)}, u32[]{:S(2)}) collective-permute-start(bf16[320,1024]{1,0:T(8,128)(2,1)S(1)} %bitcast.25), channel_id=1, source_target_pairs={{0,6},{1,7},{2,0},{3,1},{4,2},{5,3},{6,4},{7,5},{8,14},{9,15},{10,... | collective-permute-start | bytes 1966088 | tf_op jit(solution)/shard_map/ppermute | solution.py:160
  23.3 18.7 %collective-permute-start.15 = (bf16[320,1024]{1,0:T(8,128)(2,1)S(1)}, bf16[320,1024]{1,0:T(8,128)(2,1)S(1)}, u32[]{:S(2)}, u32[]{:S(2)}) collective-permute-start(bf16[320,1024]{1,0:T(8,128)(2,1)S(1)} %bitcast.26), channel_id=1, source_target_pairs={{0,1},{1,0},{2,3},{3,2},{4,5},{5,4},{6,7},{7,6},{8,9},{9,8},{10,11... | collective-permute-start | bytes 1966088 | tf_op jit(solution)/shard_map/ppermute | solution.py:160
  25.1 18.4 %collective-permute-start.3 = (bf16[320,1024]{1,0:T(8,128)(2,1)}, bf16[320,1024]{1,0:T(8,128)(2,1)S(1)}, u32[]{:S(2)}, u32[]{:S(2)}) collective-permute-start(bf16[320,1024]{1,0:T(8,128)(2,1)} %collective-permute-done.refs_3_), channel_id=1, source_target_pairs={{0,2},{1,3},{2,4},{3,5},{4,6},{5,7},{6,0},{7,1},{8,10},{9,11},{10,... | collective-permute-start | bytes 1966088 | tf_op jit(solution)/shard_map/ppermute | solution.py:160
  25.1 19.7 %collective-permute-start.16 = (bf16[320,1024]{1,0:T(8,128)(2,1)}, bf16[320,1024]{1,0:T(8,128)(2,1)}, u32[]{:S(2)}, u32[]{:S(2)}) collective-permute-start(bf16[320,1024]{1,0:T(8,128)(2,1)} %collective-permute-done.refs_3_), channel_id=1, source_target_pairs={{0,1},{1,0},{2,3},{3,2},{4,5},{5,4},{6,7},{7,6},{8,9},{9,8},{10,11... | collective-permute-start | bytes 1966088 | tf_op jit(solution)/shard_map/ppermute | solution.py:160
  38.9 8.6 %collective-permute-start.18 = (bf16[320,1024]{1,0:T(8,128)(2,1)}, bf16[320,1024]{1,0:T(8,128)(2,1)}, u32[]{:S(2)}, u32[]{:S(2)}) collective-permute-start(bf16[320,1024]{1,0:T(8,128)(2,1)} %collective-permute-done.5.refs_5_), channel_id=1, source_target_pairs={{0,1},{1,0},{2,3},{3,2},{4,5},{5,4},{6,7},{7,6},{8,9},{9,8},{10,11... | collective-permute-start | bytes 1966088 | tf_op jit(solution)/shard_map/ppermute | solution.py:160
  41.1 29.2 %collective-permute-start.1 = (bf16[320,1024]{1,0:T(8,128)(2,1)}, bf16[320,1024]{1,0:T(8,128)(2,1)S(1)}, u32[]{:S(2)}, u32[]{:S(2)}) collective-permute-start(bf16[320,1024]{1,0:T(8,128)(2,1)} %collective-permute-done.refs_3_), channel_id=1, source_target_pairs={{0,8},{1,9},{2,10},{3,11},{4,12},{5,13},{6,14},{7,15},{8,0},{9,1},... | collective-permute-start | bytes 1966088 | tf_op jit(solution)/shard_map/ppermute | solution.py:160
  42.0 1.5 %copy-start.14 = (bf16[320,1024]{1,0:T(8,128)(2,1)}, bf16[320,1024]{1,0:T(8,128)(2,1)S(1)}, u32[]{:S(2)}) copy-start(bf16[320,1024]{1,0:T(8,128)(2,1)S(1)} %collective-permute-done.15.refs_6_) | copy-start | bytes 1966084
  42.0 29.0 %collective-permute-start.6 = (bf16[320,1024]{1,0:T(8,128)(2,1)}, bf16[320,1024]{1,0:T(8,128)(2,1)S(1)}, u32[]{:S(2)}, u32[]{:S(2)}) collective-permute-start(bf16[320,1024]{1,0:T(8,128)(2,1)} %collective-permute-done.5.refs_5_), channel_id=1, source_target_pairs={{0,6},{1,7},{2,0},{3,1},{4,2},{5,3},{6,4},{7,5},{8,14},{9,15},{10,... | collective-permute-start | bytes 1966088 | tf_op jit(solution)/shard_map/ppermute | solution.py:160
  43.5 45.3 %copy-start.3 = (bf16[320,1024]{1,0:T(8,128)(2,1)}, bf16[320,1024]{1,0:T(8,128)(2,1)S(1)}, u32[]{:S(2)}) copy-start(bf16[320,1024]{1,0:T(8,128)(2,1)S(1)} %collective-permute-done.3.refs_2_) | copy-start | bytes 1966084
  43.5 28.3 %collective-permute-start.17 = (bf16[320,1024]{1,0:T(8,128)(2,1)}, bf16[320,1024]{1,0:T(8,128)(2,1)}, u32[]{:S(2)}, u32[]{:S(2)}) collective-permute-start(bf16[320,1024]{1,0:T(8,128)(2,1)} %collective-permute-done.14.refs_4_), channel_id=1, source_target_pairs={{0,1},{1,0},{2,3},{3,2},{4,5},{5,4},{6,7},{7,6},{8,9},{9,8},{10,11... | collective-permute-start | bytes 1966088 | tf_op jit(solution)/shard_map/ppermute | solution.py:160
  44.8 29.7 %collective-permute-start.4 = (bf16[96,1024]{1,0:T(8,128)(2,1)S(1)}, bf16[96,1024]{1,0:T(8,128)(2,1)S(1)}, u32[]{:S(2)}, u32[]{:S(2)}) collective-permute-start(bf16[96,1024]{1,0:T(8,128)(2,1)S(1)} %slice.13), channel_id=1, source_target_pairs={{0,8},{1,9},{2,10},{3,11},{4,12},{5,13},{6,14},{7,15},{8,0},{9,1},... | collective-permute-start | bytes 589832 | tf_op jit(solution)/shard_map/ppermute | solution.py:160
  47.5 42.5 %collective-permute-start.11 = (bf16[320,1024]{1,0:T(8,128)(2,1)S(1)}, bf16[320,1024]{1,0:T(8,128)(2,1)S(1)}, u32[]{:S(2)}, u32[]{:S(2)}) collective-permute-start(bf16[320,1024]{1,0:T(8,128)(2,1)S(1)} %collective-permute-done.3.refs_2_), channel_id=1, source_target_pairs={{0,1},{1,0},{2,3},{3,2},{4,5},{5,4},{6,7},{7,6},{8,9},{9,8},{10,11... | collective-permute-start | bytes 1966088 | tf_op jit(solution)/shard_map/ppermute | solution.py:160
  70.3 18.6 %copy-start.1 = (bf16[320,1024]{1,0:T(8,128)(2,1)}, bf16[320,1024]{1,0:T(8,128)(2,1)S(1)}, u32[]{:S(2)}) copy-start(bf16[320,1024]{1,0:T(8,128)(2,1)S(1)} %collective-permute-done.1.refs_4_) | copy-start | bytes 1966084
  70.3 20.1 %collective-permute-start.13 = (bf16[320,1024]{1,0:T(8,128)(2,1)S(1)}, bf16[320,1024]{1,0:T(8,128)(2,1)S(1)}, u32[]{:S(2)}, u32[]{:S(2)}) collective-permute-start(bf16[320,1024]{1,0:T(8,128)(2,1)S(1)} %collective-permute-done.1.refs_4_), channel_id=1, source_target_pairs={{0,1},{1,0},{2,3},{3,2},{4,5},{5,4},{6,7},{7,6},{8,9},{9,8},{10,11... | collective-permute-start | bytes 1966088 | tf_op jit(solution)/shard_map/ppermute | solution.py:160
  71.0 17.8 %copy-start.2 = (bf16[320,1024]{1,0:T(8,128)(2,1)}, bf16[320,1024]{1,0:T(8,128)(2,1)S(1)}, u32[]{:S(2)}) copy-start(bf16[320,1024]{1,0:T(8,128)(2,1)S(1)} %collective-permute-done.6.refs_3_) | copy-start | bytes 1966084
  71.0 19.3 %collective-permute-start.12 = (bf16[320,1024]{1,0:T(8,128)(2,1)S(1)}, bf16[320,1024]{1,0:T(8,128)(2,1)S(1)}, u32[]{:S(2)}, u32[]{:S(2)}) collective-permute-start(bf16[320,1024]{1,0:T(8,128)(2,1)S(1)} %collective-permute-done.6.refs_3_), channel_id=1, source_target_pairs={{0,1},{1,0},{2,3},{3,2},{4,5},{5,4},{6,7},{7,6},{8,9},{9,8},{10,11... | collective-permute-start | bytes 1966088 | tf_op jit(solution)/shard_map/ppermute | solution.py:160
  71.8 17.0 %collective-permute-start.2 = (bf16[112,1024]{1,0:T(8,128)(2,1)S(1)}, bf16[112,1024]{1,0:T(8,128)(2,1)S(1)}, u32[]{:S(2)}, u32[]{:S(2)}) collective-permute-start(bf16[112,1024]{1,0:T(8,128)(2,1)S(1)} %slice.12), channel_id=1, source_target_pairs={{0,2},{1,3},{2,4},{3,5},{4,6},{5,7},{6,0},{7,1},{8,10},{9,11},{10,... | collective-permute-start | bytes 688136 | tf_op jit(solution)/shard_map/ppermute | solution.py:160
  74.5 14.4 %copy-start.11 = (bf16[96,1024]{1,0:T(8,128)(2,1)}, bf16[96,1024]{1,0:T(8,128)(2,1)S(1)}, u32[]{:S(2)}) copy-start(bf16[96,1024]{1,0:T(8,128)(2,1)S(1)} %collective-permute-done.4.refs_3_) | copy-start | bytes 589828
  74.5 15.4 %collective-permute-start.7 = (bf16[112,1024]{1,0:T(8,128)(2,1)S(1)}, bf16[112,1024]{1,0:T(8,128)(2,1)S(1)}, u32[]{:S(2)}, u32[]{:S(2)}) collective-permute-start(bf16[112,1024]{1,0:T(8,128)(2,1)S(1)} %slice.14), channel_id=1, source_target_pairs={{0,6},{1,7},{2,0},{3,1},{4,2},{5,3},{6,4},{7,5},{8,14},{9,15},{10,... | collective-permute-start | bytes 688136 | tf_op jit(solution)/shard_map/ppermute | solution.py:160
  88.9 15.8 %copy-start.7 = (bf16[112,1024]{1,0:T(8,128)(2,1)}, bf16[112,1024]{1,0:T(8,128)(2,1)S(1)}, u32[]{:S(2)}) copy-start(bf16[112,1024]{1,0:T(8,128)(2,1)S(1)} %collective-permute-done.2.refs_2_) | copy-start | bytes 688132
  88.9 15.7 %collective-permute-start.9 = (bf16[96,1024]{1,0:T(8,128)(2,1)S(1)}, bf16[96,1024]{1,0:T(8,128)(2,1)S(1)}, u32[]{:S(2)}, u32[]{:S(2)}) collective-permute-start(bf16[96,1024]{1,0:T(8,128)(2,1)S(1)} %collective-permute-done.4.refs_3_), channel_id=1, source_target_pairs={{0,1},{1,0},{2,3},{3,2},{4,5},{5,4},{6,7},{7,6},{8,9},{9,8},{10,11... | collective-permute-start | bytes 589832 | tf_op jit(solution)/shard_map/ppermute | solution.py:160
  89.8 14.8 %copy-start.8 = (bf16[112,1024]{1,0:T(8,128)(2,1)}, bf16[112,1024]{1,0:T(8,128)(2,1)S(1)}, u32[]{:S(2)}) copy-start(bf16[112,1024]{1,0:T(8,128)(2,1)S(1)} %collective-permute-done.7.refs_4_) | copy-start | bytes 688132
  89.9 14.8 %collective-permute-start.8 = (bf16[112,1024]{1,0:T(8,128)(2,1)S(1)}, bf16[112,1024]{1,0:T(8,128)(2,1)S(1)}, u32[]{:S(2)}, u32[]{:S(2)}) collective-permute-start(bf16[112,1024]{1,0:T(8,128)(2,1)S(1)} %collective-permute-done.2.refs_2_), channel_id=1, source_target_pairs={{0,1},{1,0},{2,3},{3,2},{4,5},{5,4},{6,7},{7,6},{8,9},{9,8},{10,11... | collective-permute-start | bytes 688136 | tf_op jit(solution)/shard_map/ppermute | solution.py:160
  90.0 0.8 copy-start.4
  90.0 14.7 %collective-permute-start.10 = (bf16[112,1024]{1,0:T(8,128)(2,1)S(1)}, bf16[112,1024]{1,0:T(8,128)(2,1)S(1)}, u32[]{:S(2)}, u32[]{:S(2)}) collective-permute-start(bf16[112,1024]{1,0:T(8,128)(2,1)S(1)} %collective-permute-done.7.refs_4_), channel_id=1, source_target_pairs={{0,1},{1,0},{2,3},{3,2},{4,5},{5,4},{6,7},{7,6},{8,9},{9,8},{10,11... | collective-permute-start | bytes 688136 | tf_op jit(solution)/shard_map/ppermute | solution.py:160
  90.4 0.8 copy-start.5
  91.2 0.9 copy-start.6
  104.6 0.7 copy-start.12
  104.6 0.7 copy-start.9
  104.6 0.8 copy-start.10
  115.2 1.2 copy-start

commit v2 on v0

v2 whole, which is shorter than its diff:
```python
import math

import jax
import jax.numpy as jnp
from jax import lax
from jax.experimental import pallas as pl
from jax.experimental.pallas import tpu as pltpu
from jax.sharding import PartitionSpec as P

perturb_scale = 0.5
f32, bf16 = jnp.float32, jnp.bfloat16

D, COLS, ROWS, SHARD = 5120, 1088, 1024, 320
CHIP = 2 * SHARD
LOW = 32
TALL = COLS + LOW
NB = 256
WIDE = 384
BCOLS = 1152
PAY = 2 * WIDE + BCOLS
POPS, ZS, XS = 16, 8, 4
LAST = CHIP + 128
MIB = 2**20

IN_VMEM = pl.BlockSpec(memory_space=pltpu.VMEM)
IN_SMEM = pl.BlockSpec(memory_space=pltpu.SMEM)
ANYWHERE = pl.BlockSpec(memory_space=pl.ANY)
IN_HBM = pl.BlockSpec(memory_space=pltpu.HBM)

TP = [(y, x, c) for y in range(2) for x in range(XS) for c in range(2)]


def tp_at(y, x, c):
    return ((y % 2) * XS + x % XS) * 2 + c % 2


X_UP = [(tp_at(y, x, c), tp_at(y, x + 1, c)) for y, x, c in TP]
X_DOWN = [(tp_at(y, x, c), tp_at(y, x - 1, c)) for y, x, c in TP]
Y_SWAP = [(tp_at(y, x, c), tp_at(y + 1, x, c)) for y, x, c in TP]
CORE_SWAP = [(tp_at(y, x, c), tp_at(y, x, c + 1)) for y, x, c in TP]


Z_GROUPS = [[z * 2 + yl for z in range(ZS)] for yl in range(2)]
PAIR_SWAP = [(p, p ^ 1) for p in range(POPS)]

NEAR = ((0, 0), (0, -1), (0, 1), (1, 0))
FAR = ((0, 2), (1, 1), (1, -1), (1, 2))


def kernel_call(kernel, args, in_specs, outs, out_specs, scratch, flops, nbytes, vmem, alias=None):
    return pl.pallas_call(
        kernel,
        out_shape=[jax.ShapeDtypeStruct(shape, dtype) for shape, dtype in outs],
        in_specs=in_specs,
        out_specs=out_specs,
        scratch_shapes=scratch,
        input_output_aliases=alias or {},
        compiler_params=pltpu.CompilerParams(vmem_limit_bytes=vmem * MIB),
        cost_estimate=pl.CostEstimate(
            flops=int(flops), bytes_accessed=int(nbytes), transcendentals=0
        ),
    )(*args)


def start_all(pairs, sem):
    handles = [pltpu.make_async_copy(src, dst, sem.at[i]) for i, (src, dst) in enumerate(pairs)]
    for h in handles:
        h.start()
    return handles


def core_now():
    return lax.rem(lax.axis_index("tp"), 2)


def pair_now():
    return lax.rem(lax.axis_index("pop"), 2)


def weights_kernel(steps, w, a, b_hbm, wx, b_t, sem):
    tp = lax.axis_index("tp")
    x, y = lax.rem(tp // 2, XS), tp // (2 * XS)
    used = len(steps) * CHIP
    more = wx.shape[1] > used
    pairs = [(b_hbm, b_t)] if more else []
    for k, (dy, dx) in enumerate(steps):
        chip = lax.rem(y + dy, 2) * XS + lax.rem(x + dx + XS, XS)
        col = pl.ds(pl.multiple_of(chip * CHIP, 128), CHIP)
        here = pl.ds(k * CHIP, CHIP)
        pairs.append((w.at[:, col], wx.at[pl.ds(0, COLS), here]))
        pairs.append((a.at[:, col], wx.at[pl.ds(COLS, LOW), here]))
    handles = start_all(pairs, sem)
    if more:
        handles.pop(0).wait()
        wx[:, used:] = jnp.zeros((TALL, wx.shape[1] - used), bf16)
        wx[:COLS, used : used + LOW] = b_t[...]
    for h in handles:
        h.wait()


def weights(steps, extra, w, a, b_t, vmem):
    width = len(steps) * CHIP + extra
    (wx,) = kernel_call(
        lambda *refs: weights_kernel(steps, *refs),
        (w, a, b_t),
        [IN_HBM, ANYWHERE, ANYWHERE],
        [((TALL, width), bf16)],
        [IN_VMEM],
        [pltpu.VMEM((COLS, LOW), bf16), pltpu.SemaphoreType.DMA((2 * len(steps) + 1,))],
        0,
        4 * TALL * width,
        vmem,
    )
    return wx


def token_pairs(places, mine, other, xs):
    core = core_now()
    pairs = []
    for start, m, o in zip(places, mine, other):
        size = m.shape[0]
        m_row = pl.multiple_of(start + core * SHARD, 16)
        o_row = pl.multiple_of(start + (1 - core) * SHARD, 16)
        pairs.append((m, xs.at[pl.ds(m_row, size), :]))
        pairs.append((o, xs.at[pl.ds(o_row, size), :]))
    return pairs


def part_kernel(n, first, *refs):
    wx, mine, other = refs[0], refs[1 : 1 + n], refs[1 + n : 1 + 2 * n]
    acc, out, xs, sem = (None, *refs[-3:]) if first else refs[-4:]
    for h in start_all(token_pairs([k * CHIP for k in range(n)], mine, other, xs), sem):
        h.wait()
    depth = n * CHIP
    for j in range(ROWS // NB):
        cols = slice(j * NB, (j + 1) * NB)
        part = jnp.dot(wx[:, :depth], xs[:, cols], preferred_element_type=f32)
        out[:, cols] = part if first else acc[:, cols] + part


def part_product(wx, mine, other, acc=None):
    n = len(mine)
    first = acc is None
    args = (wx, *mine, *other) + (() if first else (acc,))
    (out,) = kernel_call(
        lambda *refs: part_kernel(n, first, *refs),
        args,
        [IN_VMEM, IN_HBM if first else IN_VMEM] + [IN_VMEM] * (len(args) - 2),
        [((TALL, ROWS), f32)],
        [IN_VMEM],
        [pltpu.VMEM((n * CHIP, ROWS), bf16), pltpu.SemaphoreType.DMA((2 * n,))],
        2 * TALL * n * CHIP * ROWS,
        2 * n * CHIP * (TALL + ROWS),
        14,
    )
    return out


def last_kernel(places, wx, *refs):
    n = len(places)
    mine, other = refs[:n], refs[n : 2 * n]
    acc, member, out, xs, act, sem = refs[2 * n :]
    handles = start_all(token_pairs(places, mine, other, xs), sem)
    off = wx.shape[1] - LAST
    rank_row = lax.broadcasted_iota(jnp.int32, (LOW, ROWS), 0) >> 2
    owned = rank_row == member[...] - lax.axis_index("pop") * 8
    xs[CHIP + LOW :, :] = jnp.zeros((LAST - CHIP - LOW, ROWS), bf16)
    for h in handles:
        h.wait()
    low = acc[COLS:, :] + jnp.dot(
        wx[COLS:, off : off + CHIP], xs[:CHIP, :], preferred_element_type=f32
    )
    scaled = low * (perturb_scale / math.sqrt(D))
    xs[CHIP : CHIP + LOW, :] = jnp.where(owned, scaled, 0.0).astype(bf16)
    done = []
    for j in range(ROWS // NB):
        cols = slice(j * NB, (j + 1) * NB)
        v = acc[:COLS, cols] + jnp.dot(wx[:COLS, off:], xs[:, cols], preferred_element_type=f32)
        half = 0.5 * v
        act[:, cols] = (half + half * jnp.tanh(half)).astype(bf16)
        copy = pltpu.make_async_copy(act.at[:, cols], out.at[:, cols], sem.at[2 * n + j])
        copy.start()
        done.append(copy)
    for copy in done:
        copy.wait()


def last_product(places, wx, mine, other, acc, member):
    n = len(places)
    args = (wx, *mine, *other, acc, member)
    (out,) = kernel_call(
        lambda *refs: last_kernel(places, *refs),
        args,
        [IN_VMEM] * len(args),
        [((COLS, ROWS), bf16)],
        [IN_HBM],
        [
            pltpu.VMEM((LAST, ROWS), bf16),
            pltpu.VMEM((COLS, ROWS), bf16),
            pltpu.SemaphoreType.DMA((2 * n + ROWS // NB,)),
        ],
        2 * TALL * CHIP * ROWS,
        2 * CHIP * (TALL + ROWS),
        12,
    )
    return out


def slices_for(pair, z):
    return pl.ds(pl.multiple_of(2 * SHARD * z + 256 * pair, 128), WIDE)


def factors_kernel(rank, a_hbm, b_hbm, a_flat, b_t, out, a, b, wide_a, wide_b, wide_s, sem):
    for h in start_all([(a_hbm, a), (b_hbm, b)], sem):
        h.wait()
    wide_s[:, BCOLS - 128 :] = jnp.zeros((LOW, 128), f32)
    for m in range(8):
        rows = slice(4 * m, 4 * m + 4)
        wide_a[rows, :] = a[m].astype(f32)
        bm = b[m].astype(f32)
        wide_b[rows, :] = bm
        fitness = 2.0 * jnp.full((4, COLS), rank[m], jnp.int32).astype(f32) / 127.0 - 1.0
        wide_s[rows, :COLS] = bm * fitness
    a_flat[...] = wide_a[...].astype(bf16)
    b_t[...] = wide_b[...].T.astype(bf16)
    scaled = wide_s[...].astype(bf16)
    pair = pair_now()
    for z in range(ZS):
        out[z, :, :WIDE] = a_flat[:, slices_for(pair, z)]
        out[z, :, WIDE : 2 * WIDE] = a_flat[:, slices_for(1 - pair, z)]
        out[z, :, 2 * WIDE :] = scaled


def pair_kernel(got, out):
    out[...] = got[:, WIDE:]


def pair_message(got):
    shape = (got.shape[0], PAY - WIDE)
    (out,) = kernel_call(
        pair_kernel, (got,), [IN_VMEM], [(shape, bf16)], [IN_VMEM], [], 0, 4 * math.prod(shape), 4
    )
    return out


def update_kernel(got, far, out, wide, up, sem):
    def outer(left, right):
        return lax.dot_general(
            left, right, (((0,), (0,)), ((), ())), preferred_element_type=f32
        )

    wide[...] = (
        outer(got[:, :WIDE], got[:, 2 * WIDE : 2 * WIDE + COLS])
        + outer(far[:, :WIDE], far[:, WIDE : WIDE + COLS])
    )
    first = pl.multiple_of(pair_now() * 64, 64)
    up[...] = (wide[pl.ds(first, SHARD), :] * (1.0 / math.sqrt(512))).astype(bf16)
    copy = pltpu.make_async_copy(up, out, sem)
    copy.start()
    copy.wait()


def body(tokens, weight, factor_a, factor_b, member_of_row, fitness_rank):
    shard = tokens.T
    w = weight.T

    send = lambda v, perm: lax.ppermute(v, "tp", perm)
    swap = lambda v: send(v, CORE_SWAP)

    low_x = send(shard, X_UP)
    high_x = send(shard, X_DOWN)
    far_y = send(shard, Y_SWAP)
    own_o = swap(shard)

    a, b_t, payload = kernel_call(
        factors_kernel,
        (fitness_rank, factor_a, factor_b),
        [IN_SMEM, IN_HBM, IN_HBM],
        [((LOW, D), bf16), ((COLS, LOW), bf16), ((ZS, LOW, PAY), bf16)],
        [IN_VMEM] * 3,
        [
            pltpu.VMEM((8, 4, D), bf16),
            pltpu.VMEM((8, 4, COLS), bf16),
            pltpu.VMEM((LOW, D), f32),
            pltpu.VMEM((LOW, COLS), f32),
            pltpu.VMEM((LOW, BCOLS), f32),
            pltpu.SemaphoreType.DMA((2,)),
        ],
        0,
        2 * LOW * (D + COLS + ZS * PAY),
        54,
    )
    got = lax.all_to_all(payload, "pop", 0, 0, axis_index_groups=Z_GROUPS, tiled=True)
    got = got.reshape(ZS * LOW, PAY)

    near_w = weights(NEAR, 0, w, a, b_t, 44)
    far_w = weights(FAR, 128, w, a, b_t, 42)

    two_x = send(low_x, X_UP)
    far_high = send(far_y, X_DOWN)
    far_low = send(low_x, Y_SWAP)
    o1 = [own_o, swap(low_x), swap(high_x), swap(far_y)]
    acc = part_product(near_w, [shard, low_x, high_x, far_y], o1)

    two_x, far_high, far_low, acc, got = lax.optimization_barrier(
        (two_x, far_high, far_low, acc, got)
    )
    e = [send(far_low[: SHARD // 2], X_UP), send(far_high[SHARD // 2 :], X_DOWN)]
    o2 = [swap(two_x), swap(far_high), swap(far_low)]
    far = lax.ppermute(pair_message(got), "pop", PAIR_SWAP)
    acc = part_product(far_w, [two_x, far_high, far_low], o2, acc)

    *e, acc = lax.optimization_barrier((*e, acc))
    oe = [swap(v) for v in e]
    act = last_product((0, SHARD // 2), far_w, e, oe, acc, member_of_row.reshape(1, ROWS))
    act, far = lax.optimization_barrier((act, far))
    (update,) = kernel_call(
        update_kernel,
        (got, far),
        [IN_VMEM] * 2,
        [((SHARD, COLS), bf16)],
        [IN_HBM],
        [
            pltpu.VMEM((WIDE, COLS), f32),
            pltpu.VMEM((SHARD, COLS), bf16),
            pltpu.SemaphoreType.DMA,
        ],
        2 * 512 * WIDE * COLS,
        2 * 512 * PAY,
        8,
    )
    return (act.T, update)


def solution(mesh):
    placed = (
        P("pop", "tp"),
        P(None, "tp"),
        P("pop", None, None),
        P("pop", None, "tp"),
        P("pop"),
        P("pop"),
    )
    return jax.shard_map(
        body,
        mesh=mesh,
        in_specs=placed,
        out_specs=(P("pop", "tp"), P("pop", "tp")),
        check_vma=False,
    )
```

time: 331 us -> 73.9 us (0.22)
  waiting for transfers between devices: 282 us -> 9.26 us
  Pallas kernels: 0 us -> 30.7 us
  matrix products: 30.5 us -> 0 us
  starting transfers between devices: 0.12 us -> 28.7 us
  between operations: 13.8 us -> 0.96 us
    all_gather x3 -> x0, waiting for transfers between devices: 280 us -> none  [the longest x1 121 us: body(): lax.all_gather(factor_a, 'pop', axis=0, tiled=True)]
    pallas_call x0 -> x8, Pallas kernels: none -> 30.7 us  [kernel_call(): pl.pallas_call(kernel, out_shape=[jax.ShapeDtypeStruct(shape, dtype) for...]
    dot_general x3 -> x0, matrix products: 30.5 us -> none  [the longest x1 19.2 us: body(): preact = jnp.dot(segment, weight, preferred_element_type=jnp.float32)]
    ppermute x0 -> x18, starting transfers between devices: none -> 20.5 us  [the longest x17 20 us: body(): send = lambda v, perm: lax.ppermute(v, 'tp', perm)]
    all_to_all x0 -> x1, starting transfers between devices: none -> 8.2 us  [body(): lax.all_to_all(payload, 'pop', 0, 0, axis_index_groups=Z_GROUPS, tiled=True)]
    ppermute x0 -> x18, waiting for transfers between devices: none -> 6.68 us  [the longest x1 4.01 us: body(): far = lax.ppermute(pair_message(got), 'pop', PAIR_SWAP)]
    unnamed x4 -> x16, local copies, waits for them, and re-layouts: 0.01 us -> 4.02 us
  transfers between devices with their start and end apart: 3 -> 19, of which waited for: 3 -> 5; matrix products, arithmetic and copies ran while one was open for 2% -> 0% of each run, Pallas kernels for 0% -> 39%
where the time goes in v2:
time: 73.9 us; the launch traced here: 73.7 us
  Pallas kernels  30.7 us (42%)
  starting transfers between devices  28.7 us (39%)
  waiting for transfers between devices  9.26 us (13%)
  local copies, waits for them, and re-layouts  4.07 us (6%)
  between operations  0.96 us (1%)
    pallas_call x8, Pallas kernels, kernel_call(): pl.pallas_call(kernel, out_shape=[jax.ShapeDtypeStruct(shape, dtype) for...  30.7 us
    ppermute x17, starting transfers between devices, body(): send = lambda v, perm: lax.ppermute(v, 'tp', perm)  20 us
    all_to_all x1, starting transfers between devices, body(): lax.all_to_all(payload, 'pop', 0, 0, axis_index_groups=Z_GROUPS, tiled=True)  8.2 us
    unnamed x16, local copies, waits for them, and re-layouts  4.02 us
    ppermute x1, waiting for transfers between devices, body(): far = lax.ppermute(pair_message(got), 'pop', PAIR_SWAP)  4.01 us
    ppermute x17, waiting for transfers between devices, body(): send = lambda v, perm: lax.ppermute(v, 'tp', perm)  2.67 us
    all_to_all x1, waiting for transfers between devices, body(): lax.all_to_all(payload, 'pop', 0, 0, axis_index_groups=Z_GROUPS, tiled=True)  2.58 us
  transfers between devices with their start and end apart: 19, of which 5 were waited for; matrix products, arithmetic and copies ran while one was open for 0% of the time, Pallas kernels for 39%

profile of v2, /device:TPU:1, one launch (start us, length us, event | category | flops | bytes accessed | tf_op | source)
XLA Modules:
  0.0 73.7 jit_solution(13338505496098228837)
XLA Ops:
  0.6 2.1 %collective-permute-start = (bf16[320,1024]{1,0:T(8,128)(2,1)}, bf16[320,1024]{1,0:T(8,128)(2,1)}, u32[]{:S(2)}, u32[]{:S(2)}) collective-permute-start(bf16[320,1024]{1,0:T(8,128)(2,1)} %bitcast.8), channel_id=1, source_target_pairs={{0,2},{1,3},{2,4},{3,5},{4,6},{5,7},{6,0},{7,1},{8,10},{9,11},{10,... | collective-permute-start | bytes 1966088 | tf_op jit(solution)/shard_map/ppermute | solution.py:267
  2.7 2.9 %collective-permute-start.2 = (bf16[320,1024]{1,0:T(8,128)(2,1)}, bf16[320,1024]{1,0:T(8,128)(2,1)}, u32[]{:S(2)}, u32[]{:S(2)}) collective-permute-start(bf16[320,1024]{1,0:T(8,128)(2,1)} %bitcast.9), channel_id=1, source_target_pairs={{0,8},{1,9},{2,10},{3,11},{4,12},{5,13},{6,14},{7,15},{8,0},{9,1},... | collective-permute-start | bytes 1966088 | tf_op jit(solution)/shard_map/ppermute | solution.py:267
  5.7 1.5 %collective-permute-start.5 = (bf16[320,1024]{1,0:T(8,128)(2,1)}, bf16[320,1024]{1,0:T(8,128)(2,1)}, u32[]{:S(2)}, u32[]{:S(2)}) collective-permute-start(bf16[320,1024]{1,0:T(8,128)(2,1)} %bitcast.10), channel_id=1, source_target_pairs={{0,6},{1,7},{2,0},{3,1},{4,2},{5,3},{6,4},{7,5},{8,14},{9,15},{10,... | collective-permute-start | bytes 1966088 | tf_op jit(solution)/shard_map/ppermute | solution.py:267
  7.1 3.0 %shard_map.77 = (bf16[32,5120]{1,0:T(8,128)(2,1)}, bf16[1088,32]{1,0:T(8,128)(2,1)}, bf16[8,32,1920]{2,1,0:T(8,128)(2,1)}) custom-call(s32[8]{0:T(128)} %rank.1, bf16[8,4,5120]{2,1,0:T(4,128)(2,1)} %a_hbm.1, bf16[8,4,1088]{2,1,0:T(4,128)(2,1)} %b_hbm.1), custom_call_target="tpu_custom_call" | custom-call | bytes 1380352 | tf_op jit(solution)/shard_map/pallas_call | solution.py:51
  10.2 8.2 %all-to-all-start = ((bf16[8,32,1920]{2,1,0:T(8,128)(2,1)}), bf16[8,32,1920]{2,1,0:T(8,128)(2,1)S(1)}, u32[]{:S(2)}, u32[]{:S(2)}) async-start(bf16[8,32,1920]{2,1,0:T(8,128)(2,1)} %get-tuple-element.17), calls=%async_computation | async-start | bytes 1966080 | tf_op jit(solution)/shard_map/all_to_all | solution.py:293
  18.4 1.8 %collective-permute-start.6 = (bf16[320,1024]{1,0:T(8,128)(2,1)}, bf16[320,1024]{1,0:T(8,128)(2,1)S(1)}, u32[]{:S(2)}, u32[]{:S(2)}) collective-permute-start(bf16[320,1024]{1,0:T(8,128)(2,1)} %bitcast.11), channel_id=1, source_target_pairs={{0,1},{1,0},{2,3},{3,2},{4,5},{5,4},{6,7},{7,6},{8,9},{9,8},{10,11... | collective-permute-start | bytes 1966088 | tf_op jit(solution)/shard_map/ppermute | solution.py:267
  20.2 0.0 collective-permute-done.refs_2_
  20.2 0.1 collective-permute-start.7
  20.3 0.0 collective-permute-done.2.refs_4_
  20.3 1.5 %collective-permute-start.9 = (bf16[320,1024]{1,0:T(8,128)(2,1)}, bf16[320,1024]{1,0:T(8,128)(2,1)S(1)}, u32[]{:S(2)}, u32[]{:S(2)}) collective-permute-start(bf16[320,1024]{1,0:T(8,128)(2,1)} %collective-permute-done.2.refs_4_), channel_id=1, source_target_pairs={{0,1},{1,0},{2,3},{3,2},{4,5},{5,4},{6,7},{7,6},{8,9},{9,8},{10,11... | collective-permute-start | bytes 1966088 | tf_op jit(solution)/shard_map/ppermute | solution.py:267
  21.7 0.0 collective-permute-done.5.refs_3_
  21.7 1.4 %collective-permute-start.8 = (bf16[320,1024]{1,0:T(8,128)(2,1)}, bf16[320,1024]{1,0:T(8,128)(2,1)S(1)}, u32[]{:S(2)}, u32[]{:S(2)}) collective-permute-start(bf16[320,1024]{1,0:T(8,128)(2,1)} %collective-permute-done.5.refs_3_), channel_id=1, source_target_pairs={{0,1},{1,0},{2,3},{3,2},{4,5},{5,4},{6,7},{7,6},{8,9},{9,8},{10,11... | collective-permute-start | bytes 1966088 | tf_op jit(solution)/shard_map/ppermute | solution.py:267
  23.1 1.2 %collective-permute-start.1 = (bf16[320,1024]{1,0:T(8,128)(2,1)}, bf16[320,1024]{1,0:T(8,128)(2,1)S(1)}, u32[]{:S(2)}, u32[]{:S(2)}) collective-permute-start(bf16[320,1024]{1,0:T(8,128)(2,1)} %collective-permute-done.refs_2_), channel_id=1, source_target_pairs={{0,2},{1,3},{2,4},{3,5},{4,6},{5,7},{6,0},{7,1},{8,10},{9,11},{10,... | collective-permute-start | bytes 1966088 | tf_op jit(solution)/shard_map/ppermute | solution.py:267
  24.3 0.0 collective-permute-done.6.refs_5_
  24.3 1.5 %collective-permute-start.4 = (bf16[320,1024]{1,0:T(8,128)(2,1)}, bf16[320,1024]{1,0:T(8,128)(2,1)S(1)}, u32[]{:S(2)}, u32[]{:S(2)}) collective-permute-start(bf16[320,1024]{1,0:T(8,128)(2,1)} %collective-permute-done.refs_2_), channel_id=1, source_target_pairs={{0,8},{1,9},{2,10},{3,11},{4,12},{5,13},{6,14},{7,15},{8,0},{9,1},... | collective-permute-start | bytes 1966088 | tf_op jit(solution)/shard_map/ppermute | solution.py:267
  25.9 0.0 collective-permute-done.7.refs_6_
  25.9 1.5 %collective-permute-start.3 = (bf16[320,1024]{1,0:T(8,128)(2,1)}, bf16[320,1024]{1,0:T(8,128)(2,1)S(1)}, u32[]{:S(2)}, u32[]{:S(2)}) collective-permute-start(bf16[320,1024]{1,0:T(8,128)(2,1)} %collective-permute-done.2.refs_4_), channel_id=1, source_target_pairs={{0,6},{1,7},{2,0},{3,1},{4,2},{5,3},{6,4},{7,5},{8,14},{9,15},{10,... | collective-permute-start | bytes 1966088 | tf_op jit(solution)/shard_map/ppermute | solution.py:267
  27.3 1.0 %copy-done.2 = bf16[32,5120]{1,0:T(8,128)(2,1)S(1)} copy-done((bf16[32,5120]{1,0:T(8,128)(2,1)S(1)}, bf16[32,5120]{1,0:T(8,128)(2,1)}, u32[]{:S(2)}) %copy-start.2) | copy-done | bytes 327704
  28.3 1.0 %copy-done.4 = bf16[1088,32]{1,0:T(8,128)(2,1)S(1)} copy-done((bf16[1088,32]{1,0:T(8,128)(2,1)S(1)}, bf16[1088,32]{1,0:T(8,128)(2,1)}, u32[]{:S(2)}) %copy-start.4) | copy-done | bytes 69656
  29.3 2.8 %shard_map.79.refs_0_ = bf16[1120,2560]{1,0:T(8,128)(2,1)S(1)} custom-call(bf16[1088,5120]{1,0:T(8,128)(2,1)} %bitcast.13, bf16[32,5120]{1,0:T(8,128)(2,1)S(1)} %copy-done.2, bf16[1088,32]{1,0:T(8,128)(2,1)S(1)} %copy-done.4), custom_call_target="tpu_custom_call" | custom-call | bytes 11468800 | tf_op jit(solution)/shard_map/pallas_call | solution.py:51
  32.0 0.0 copy-start.3
  32.1 0.0 collective-permute-done.9.refs_8_
  32.1 0.0 collective-permute-done.8.refs_7_
  32.1 9.4 %shard_map.80.refs_7_ = f32[1120,1024]{1,0:T(8,128)S(1)} custom-call(bf16[1120,2560]{1,0:T(8,128)(2,1)S(1)} %shard_map.79.refs_0_, bf16[320,1024]{1,0:T(8,128)(2,1)S(1)} %bitcast.12, bf16[320,1024]{1,0:T(8,128)(2,1)} %collective-permute-done.refs_2_, bf16[320,1024]{1,0:T(8,128)(2,1)} %collective-permute-done.5.refs_3_, ...), custom_call_target="tpu_custom_call" | custom-call | flops 5872025600 | bytes 10977280 | tf_op jit(solution)/shard_map/pallas_call | solution.py:51
  41.5 2.1 %copy-done = f32[1120,1024]{1,0:T(8,128)} copy-done((f32[1120,1024]{1,0:T(8,128)}, f32[1120,1024]{1,0:T(8,128)S(1)}, u32[]{:S(2)}) %copy-start) | copy-done | bytes 4587544
  43.6 0.0 collective-permute-done.1.refs_1_
  43.6 0.0 collective-permute-done.3.refs_2_
  43.6 2.6 %all-to-all-done = bf16[8,32,1920]{2,1,0:T(8,128)(2,1)S(1)} async-done(((bf16[8,32,1920]{2,1,0:T(8,128)(2,1)}), bf16[8,32,1920]{2,1,0:T(8,128)(2,1)S(1)}, u32[]{:S(2)}, u32[]{:S(2)}) %all-to-all-start) | async-done | bytes 983072 | tf_op jit(solution)/shard_map/all_to_all | solution.py:293
  46.1 0.5 collective-permute-start.13
  46.6 0.0 collective-permute-start.14
  46.7 0.5 collective-permute-start.12
  47.2 2.9 %shard_map.78.refs_0_ = bf16[1120,2688]{1,0:T(8,128)(2,1)S(1)} custom-call(bf16[1088,5120]{1,0:T(8,128)(2,1)} %bitcast.14, bf16[32,5120]{1,0:T(8,128)(2,1)S(1)} %copy-done.3, bf16[1088,32]{1,0:T(8,128)(2,1)S(1)} %copy-done.5), custom_call_target="tpu_custom_call" | custom-call | bytes 12042240 | tf_op jit(solution)/shard_map/pallas_call | solution.py:51
  50.1 0.1 collective-permute-start.10
  50.2 2.7 %collective-permute-start.11 = (bf16[160,1024]{1,0:T(8,128)(2,1)S(1)}, bf16[160,1024]{1,0:T(8,128)(2,1)S(1)}, u32[]{:S(2)}, u32[]{:S(2)}) collective-permute-start(bf16[160,1024]{1,0:T(8,128)(2,1)S(1)} %slice.7), channel_id=1, source_target_pairs={{0,6},{1,7},{2,0},{3,1},{4,2},{5,3},{6,4},{7,5},{8,14},{9,15},{10,... | collective-permute-start | bytes 983048 | tf_op jit(solution)/shard_map/ppermute | solution.py:267
  52.9 0.1 shard_map.83
  52.9 0.0 copy-start.6
  53.0 0.5 collective-permute-start.17
  53.4 0.0 collective-permute-done.14.refs_6_
  53.5 6.3 %shard_map.81.refs_5_ = f32[1120,1024]{1,0:T(8,128)S(1)} custom-call(bf16[1120,2688]{1,0:T(8,128)(2,1)S(1)} %shard_map.78.refs_0_, bf16[320,1024]{1,0:T(8,128)(2,1)S(1)} %collective-permute-done.1.refs_1_, bf16[320,1024]{1,0:T(8,128)(2,1)S(1)} %collective-permute-done.3.refs_2_, bf16[320,1024]{1,0:T(8,128)(2,1)S(1)} %collective-permute-done.4.refs_3_, ...), custom_call_target="tpu_custom_call" | custom-call | flops 4404019200 | bytes 8232960 | tf_op jit(solution)/shard_map/pallas_call | solution.py:51
  59.8 0.9 %collective-permute-done.10.refs_1_ = bf16[160,1024]{1,0:T(8,128)(2,1)S(1)} collective-permute-done((bf16[160,1024]{1,0:T(8,128)(2,1)S(1)}, bf16[160,1024]{1,0:T(8,128)(2,1)S(1)}, u32[]{:S(2)}, u32[]{:S(2)}) %collective-permute-start.10) | collective-permute-done | bytes 327712 | tf_op jit(solution)/shard_map/ppermute | solution.py:267
  60.7 0.0 collective-permute-done.11.refs_2_
  60.7 0.8 %collective-permute-start.15 = (bf16[160,1024]{1,0:T(8,128)(2,1)S(1)}, bf16[160,1024]{1,0:T(8,128)(2,1)S(1)}, u32[]{:S(2)}, u32[]{:S(2)}) collective-permute-start(bf16[160,1024]{1,0:T(8,128)(2,1)S(1)} %collective-permute-done.10.refs_1_), channel_id=1, source_target_pairs={{0,1},{1,0},{2,3},{3,2},{4,5},{5,4},{6,7},{7,6},{8,9},{9,8},{10,11... | collective-permute-start | bytes 983048 | tf_op jit(solution)/shard_map/ppermute | solution.py:267
  61.5 0.0 collective-permute-start.16
  61.5 1.3 %collective-permute-done.15.refs_3_ = bf16[160,1024]{1,0:T(8,128)(2,1)S(1)} collective-permute-done((bf16[160,1024]{1,0:T(8,128)(2,1)S(1)}, bf16[160,1024]{1,0:T(8,128)(2,1)S(1)}, u32[]{:S(2)}, u32[]{:S(2)}) %collective-permute-start.15) | collective-permute-done | bytes 327712 | tf_op jit(solution)/shard_map/ppermute | solution.py:267
  62.8 0.5 collective-permute-done.16.refs_4_
  63.3 4.2 %shard_map.82 = bf16[1088,1024]{1,0:T(8,128)(2,1)} custom-call(bf16[1120,2688]{1,0:T(8,128)(2,1)S(1)} %shard_map.78.refs_0_, bf16[160,1024]{1,0:T(8,128)(2,1)S(1)} %collective-permute-done.10.refs_1_, bf16[160,1024]{1,0:T(8,128)(2,1)S(1)} %collective-permute-done.11.refs_2_, bf16[160,1024]{1,0:T(8,128)(2,1)S(1)} %collective-permute-done.15.refs_3_, ...), custom_call_target="tpu_custom_call" | custom-call | flops 1468006400 | bytes 2744320 | tf_op jit(solution)/shard_map/pallas_call | solution.py:51
  67.5 4.0 %collective-permute-done.17.far = bf16[256,1536]{1,0:T(8,128)(2,1)S(1)} collective-permute-done((bf16[256,1536]{1,0:T(8,128)(2,1)S(1)}, bf16[256,1536]{1,0:T(8,128)(2,1)S(1)}, u32[]{:S(2)}, u32[]{:S(2)}) %collective-permute-start.17) | collective-permute-done | bytes 786464 | tf_op jit(solution)/shard_map/ppermute | solution.py:310
  71.5 2.0 %shard_map.84 = bf16[320,1088]{1,0:T(8,128)(2,1)} custom-call(bf16[256,1920]{1,0:T(8,128)(2,1)S(1)} %bitcast.6, bf16[256,1536]{1,0:T(8,128)(2,1)S(1)} %collective-permute-done.17.far), custom_call_target="tpu_custom_call" | custom-call | flops 427819008 | bytes 1966080 | tf_op jit(solution)/shard_map/pallas_call | solution.py:51
  (16 shorter events, 0.1 us)
Async XLA Ops:
  0.6 19.5 %collective-permute-start = (bf16[320,1024]{1,0:T(8,128)(2,1)}, bf16[320,1024]{1,0:T(8,128)(2,1)}, u32[]{:S(2)}, u32[]{:S(2)}) collective-permute-start(bf16[320,1024]{1,0:T(8,128)(2,1)} %bitcast.8), channel_id=1, source_target_pairs={{0,2},{1,3},{2,4},{3,5},{4,6},{5,7},{6,0},{7,1},{8,10},{9,11},{10,... | collective-permute-start | bytes 1966088 | tf_op jit(solution)/shard_map/ppermute | solution.py:267
  2.7 17.5 %collective-permute-start.2 = (bf16[320,1024]{1,0:T(8,128)(2,1)}, bf16[320,1024]{1,0:T(8,128)(2,1)}, u32[]{:S(2)}, u32[]{:S(2)}) collective-permute-start(bf16[320,1024]{1,0:T(8,128)(2,1)} %bitcast.9), channel_id=1, source_target_pairs={{0,8},{1,9},{2,10},{3,11},{4,12},{5,13},{6,14},{7,15},{8,0},{9,1},... | collective-permute-start | bytes 1966088 | tf_op jit(solution)/shard_map/ppermute | solution.py:267
  5.7 16.1 %collective-permute-start.5 = (bf16[320,1024]{1,0:T(8,128)(2,1)}, bf16[320,1024]{1,0:T(8,128)(2,1)}, u32[]{:S(2)}, u32[]{:S(2)}) collective-permute-start(bf16[320,1024]{1,0:T(8,128)(2,1)} %bitcast.10), channel_id=1, source_target_pairs={{0,6},{1,7},{2,0},{3,1},{4,2},{5,3},{6,4},{7,5},{8,14},{9,15},{10,... | collective-permute-start | bytes 1966088 | tf_op jit(solution)/shard_map/ppermute | solution.py:267
  10.2 36.0 %all-to-all-start = ((bf16[8,32,1920]{2,1,0:T(8,128)(2,1)}), bf16[8,32,1920]{2,1,0:T(8,128)(2,1)S(1)}, u32[]{:S(2)}, u32[]{:S(2)}) async-start(bf16[8,32,1920]{2,1,0:T(8,128)(2,1)} %get-tuple-element.17), calls=%async_computation | async-start | bytes 1966080 | tf_op jit(solution)/shard_map/all_to_all | solution.py:293
  18.4 6.0 %collective-permute-start.6 = (bf16[320,1024]{1,0:T(8,128)(2,1)}, bf16[320,1024]{1,0:T(8,128)(2,1)S(1)}, u32[]{:S(2)}, u32[]{:S(2)}) collective-permute-start(bf16[320,1024]{1,0:T(8,128)(2,1)} %bitcast.11), channel_id=1, source_target_pairs={{0,1},{1,0},{2,3},{3,2},{4,5},{5,4},{6,7},{7,6},{8,9},{9,8},{10,11... | collective-permute-start | bytes 1966088 | tf_op jit(solution)/shard_map/ppermute | solution.py:267
  20.2 5.7 %collective-permute-start.7 = (bf16[320,1024]{1,0:T(8,128)(2,1)}, bf16[320,1024]{1,0:T(8,128)(2,1)S(1)}, u32[]{:S(2)}, u32[]{:S(2)}) collective-permute-start(bf16[320,1024]{1,0:T(8,128)(2,1)} %collective-permute-done.refs_2_), channel_id=1, source_target_pairs={{0,1},{1,0},{2,3},{3,2},{4,5},{5,4},{6,7},{7,6},{8,9},{9,8},{10,11... | collective-permute-start | bytes 1966088 | tf_op jit(solution)/shard_map/ppermute | solution.py:267
  20.3 11.8 %collective-permute-start.9 = (bf16[320,1024]{1,0:T(8,128)(2,1)}, bf16[320,1024]{1,0:T(8,128)(2,1)S(1)}, u32[]{:S(2)}, u32[]{:S(2)}) collective-permute-start(bf16[320,1024]{1,0:T(8,128)(2,1)} %collective-permute-done.2.refs_4_), channel_id=1, source_target_pairs={{0,1},{1,0},{2,3},{3,2},{4,5},{5,4},{6,7},{7,6},{8,9},{9,8},{10,11... | collective-permute-start | bytes 1966088 | tf_op jit(solution)/shard_map/ppermute | solution.py:267
  21.7 10.3 %collective-permute-start.8 = (bf16[320,1024]{1,0:T(8,128)(2,1)}, bf16[320,1024]{1,0:T(8,128)(2,1)S(1)}, u32[]{:S(2)}, u32[]{:S(2)}) collective-permute-start(bf16[320,1024]{1,0:T(8,128)(2,1)} %collective-permute-done.5.refs_3_), channel_id=1, source_target_pairs={{0,1},{1,0},{2,3},{3,2},{4,5},{5,4},{6,7},{7,6},{8,9},{9,8},{10,11... | collective-permute-start | bytes 1966088 | tf_op jit(solution)/shard_map/ppermute | solution.py:267
  23.1 20.4 %collective-permute-start.1 = (bf16[320,1024]{1,0:T(8,128)(2,1)}, bf16[320,1024]{1,0:T(8,128)(2,1)S(1)}, u32[]{:S(2)}, u32[]{:S(2)}) collective-permute-start(bf16[320,1024]{1,0:T(8,128)(2,1)} %collective-permute-done.refs_2_), channel_id=1, source_target_pairs={{0,2},{1,3},{2,4},{3,5},{4,6},{5,7},{6,0},{7,1},{8,10},{9,11},{10,... | collective-permute-start | bytes 1966088 | tf_op jit(solution)/shard_map/ppermute | solution.py:267
  24.3 19.2 %collective-permute-start.4 = (bf16[320,1024]{1,0:T(8,128)(2,1)}, bf16[320,1024]{1,0:T(8,128)(2,1)S(1)}, u32[]{:S(2)}, u32[]{:S(2)}) collective-permute-start(bf16[320,1024]{1,0:T(8,128)(2,1)} %collective-permute-done.refs_2_), channel_id=1, source_target_pairs={{0,8},{1,9},{2,10},{3,11},{4,12},{5,13},{6,14},{7,15},{8,0},{9,1},... | collective-permute-start | bytes 1966088 | tf_op jit(solution)/shard_map/ppermute | solution.py:267
  25.9 17.7 %collective-permute-start.3 = (bf16[320,1024]{1,0:T(8,128)(2,1)}, bf16[320,1024]{1,0:T(8,128)(2,1)S(1)}, u32[]{:S(2)}, u32[]{:S(2)}) collective-permute-start(bf16[320,1024]{1,0:T(8,128)(2,1)} %collective-permute-done.2.refs_4_), channel_id=1, source_target_pairs={{0,6},{1,7},{2,0},{3,1},{4,2},{5,3},{6,4},{7,5},{8,14},{9,15},{10,... | collective-permute-start | bytes 1966088 | tf_op jit(solution)/shard_map/ppermute | solution.py:267
  27.3 1.0 %copy-start.2 = (bf16[32,5120]{1,0:T(8,128)(2,1)S(1)}, bf16[32,5120]{1,0:T(8,128)(2,1)}, u32[]{:S(2)}) copy-start(bf16[32,5120]{1,0:T(8,128)(2,1)} %get-tuple-element.15.refs_1_) | copy-start | bytes 983044
  28.3 1.0 %copy-start.4 = (bf16[1088,32]{1,0:T(8,128)(2,1)S(1)}, bf16[1088,32]{1,0:T(8,128)(2,1)}, u32[]{:S(2)}) copy-start(bf16[1088,32]{1,0:T(8,128)(2,1)} %get-tuple-element.16.refs_2_) | copy-start | bytes 208900
  29.3 2.8 %copy-start.7 = (bf16[1024,320]{0,1:T(8,128)(2,1)S(1)}, bf16[1024,320]{0,1:T(8,128)(2,1)}, u32[]{:S(2)}) copy-start(bf16[1024,320]{0,1:T(8,128)(2,1)} %param.6) | copy-start | bytes 1966084
  32.0 15.1 %copy-start.3 = (bf16[32,5120]{1,0:T(8,128)(2,1)S(1)}, bf16[32,5120]{1,0:T(8,128)(2,1)}, u32[]{:S(2)}) copy-start(bf16[32,5120]{1,0:T(8,128)(2,1)} %get-tuple-element.15.refs_1_) | copy-start | bytes 983044
  32.0 15.1 %copy-start.5 = (bf16[1088,32]{1,0:T(8,128)(2,1)S(1)}, bf16[1088,32]{1,0:T(8,128)(2,1)}, u32[]{:S(2)}) copy-start(bf16[1088,32]{1,0:T(8,128)(2,1)} %get-tuple-element.16.refs_2_) | copy-start | bytes 208900
  41.5 2.1 %copy-start = (f32[1120,1024]{1,0:T(8,128)}, f32[1120,1024]{1,0:T(8,128)S(1)}, u32[]{:S(2)}) copy-start(f32[1120,1024]{1,0:T(8,128)S(1)} %shard_map.80.refs_7_) | copy-start | bytes 13762564
  46.1 6.8 %collective-permute-start.13 = (bf16[320,1024]{1,0:T(8,128)(2,1)S(1)}, bf16[320,1024]{1,0:T(8,128)(2,1)S(1)}, u32[]{:S(2)}, u32[]{:S(2)}) collective-permute-start(bf16[320,1024]{1,0:T(8,128)(2,1)S(1)} %collective-permute-done.3.refs_2_), channel_id=1, source_target_pairs={{0,1},{1,0},{2,3},{3,2},{4,5},{5,4},{6,7},{7,6},{8,9},{9,8},{10,11... | collective-permute-start | bytes 1966088 | tf_op jit(solution)/shard_map/ppermute | solution.py:267
  46.6 6.8 %collective-permute-start.14 = (bf16[320,1024]{1,0:T(8,128)(2,1)S(1)}, bf16[320,1024]{1,0:T(8,128)(2,1)S(1)}, u32[]{:S(2)}, u32[]{:S(2)}) collective-permute-start(bf16[320,1024]{1,0:T(8,128)(2,1)S(1)} %collective-permute-done.4.refs_3_), channel_id=1, source_target_pairs={{0,1},{1,0},{2,3},{3,2},{4,5},{5,4},{6,7},{7,6},{8,9},{9,8},{10,11... | collective-permute-start | bytes 1966088 | tf_op jit(solution)/shard_map/ppermute | solution.py:267
  46.7 6.8 %collective-permute-start.12 = (bf16[320,1024]{1,0:T(8,128)(2,1)S(1)}, bf16[320,1024]{1,0:T(8,128)(2,1)S(1)}, u32[]{:S(2)}, u32[]{:S(2)}) collective-permute-start(bf16[320,1024]{1,0:T(8,128)(2,1)S(1)} %collective-permute-done.1.refs_1_), channel_id=1, source_target_pairs={{0,1},{1,0},{2,3},{3,2},{4,5},{5,4},{6,7},{7,6},{8,9},{9,8},{10,11... | collective-permute-start | bytes 1966088 | tf_op jit(solution)/shard_map/ppermute | solution.py:267
  47.2 6.3 %copy-start.1 = (f32[1120,1024]{1,0:T(8,128)S(1)}, f32[1120,1024]{1,0:T(8,128)}, u32[]{:S(2)}) copy-start(f32[1120,1024]{1,0:T(8,128)} %copy-done) | copy-start | bytes 13762564
  50.1 10.6 %collective-permute-start.10 = (bf16[160,1024]{1,0:T(8,128)(2,1)S(1)}, bf16[160,1024]{1,0:T(8,128)(2,1)S(1)}, u32[]{:S(2)}, u32[]{:S(2)}) collective-permute-start(bf16[160,1024]{1,0:T(8,128)(2,1)S(1)} %slice.6), channel_id=1, source_target_pairs={{0,2},{1,3},{2,4},{3,5},{4,6},{5,7},{6,0},{7,1},{8,10},{9,11},{10,... | collective-permute-start | bytes 983048 | tf_op jit(solution)/shard_map/ppermute | solution.py:267
  50.2 10.5 %collective-permute-start.11 = (bf16[160,1024]{1,0:T(8,128)(2,1)S(1)}, bf16[160,1024]{1,0:T(8,128)(2,1)S(1)}, u32[]{:S(2)}, u32[]{:S(2)}) collective-permute-start(bf16[160,1024]{1,0:T(8,128)(2,1)S(1)} %slice.7), channel_id=1, source_target_pairs={{0,6},{1,7},{2,0},{3,1},{4,2},{5,3},{6,4},{7,5},{8,14},{9,15},{10,... | collective-permute-start | bytes 983048 | tf_op jit(solution)/shard_map/ppermute | solution.py:267
  52.9 10.3 %copy-start.6 = (s32[1024]{0:T(1024)S(1)}, s32[1024]{0:T(1024)}, u32[]{:S(2)}) copy-start(s32[1024]{0:T(1024)} %param.10) | copy-start | bytes 12292
  53.0 18.6 %collective-permute-start.17 = (bf16[256,1536]{1,0:T(8,128)(2,1)S(1)}, bf16[256,1536]{1,0:T(8,128)(2,1)S(1)}, u32[]{:S(2)}, u32[]{:S(2)}) collective-permute-start(bf16[256,1536]{1,0:T(8,128)(2,1)S(1)} %shard_map.83), channel_id=1, source_target_pairs={{0,16},{16,0},{32,48},{48,32},{64,80},{80,64},{96,112},{112,96},{1... | collective-permute-start | bytes 2359304 | tf_op jit(solution)/shard_map/ppermute | solution.py:310
  60.7 2.1 %collective-permute-start.15 = (bf16[160,1024]{1,0:T(8,128)(2,1)S(1)}, bf16[160,1024]{1,0:T(8,128)(2,1)S(1)}, u32[]{:S(2)}, u32[]{:S(2)}) collective-permute-start(bf16[160,1024]{1,0:T(8,128)(2,1)S(1)} %collective-permute-done.10.refs_1_), channel_id=1, source_target_pairs={{0,1},{1,0},{2,3},{3,2},{4,5},{5,4},{6,7},{7,6},{8,9},{9,8},{10,11... | collective-permute-start | bytes 983048 | tf_op jit(solution)/shard_map/ppermute | solution.py:267
  61.5 1.7 %collective-permute-start.16 = (bf16[160,1024]{1,0:T(8,128)(2,1)S(1)}, bf16[160,1024]{1,0:T(8,128)(2,1)S(1)}, u32[]{:S(2)}, u32[]{:S(2)}) collective-permute-start(bf16[160,1024]{1,0:T(8,128)(2,1)S(1)} %collective-permute-done.11.refs_2_), channel_id=1, source_target_pairs={{0,1},{1,0},{2,3},{3,2},{4,5},{5,4},{6,7},{7,6},{8,9},{9,8},{10,11... | collective-permute-start | bytes 983048 | tf_op jit(solution)/shard_map/ppermute | solution.py:267

commit v3 on v2

--- a/solution.py
+++ b/solution.py
@@ -77,12 +77,13 @@
     return lax.rem(lax.axis_index("pop"), 2)
 
 
-def weights_kernel(steps, w, a, b_hbm, wx, b_t, sem):
+def weights_kernel(steps, w, a, *refs):
+    more = len(refs) > 2
+    wx, sem = (refs[1], refs[3]) if more else refs
     tp = lax.axis_index("tp")
     x, y = lax.rem(tp // 2, XS), tp // (2 * XS)
     used = len(steps) * CHIP
-    more = wx.shape[1] > used
-    pairs = [(b_hbm, b_t)] if more else []
+    pairs = [(refs[0], refs[2])] if more else []
     for k, (dy, dx) in enumerate(steps):
         chip = lax.rem(y + dy, 2) * XS + lax.rem(x + dx + XS, XS)
         col = pl.ds(pl.multiple_of(chip * CHIP, 128), CHIP)
@@ -93,20 +94,22 @@
     if more:
         handles.pop(0).wait()
         wx[:, used:] = jnp.zeros((TALL, wx.shape[1] - used), bf16)
-        wx[:COLS, used : used + LOW] = b_t[...]
+        wx[:COLS, used : used + LOW] = refs[2][...]
     for h in handles:
         h.wait()
 
 
-def weights(steps, extra, w, a, b_t, vmem):
+def weights(steps, extra, w, a, vmem, b_t=None):
+    more = b_t is not None
     width = len(steps) * CHIP + extra
     (wx,) = kernel_call(
         lambda *refs: weights_kernel(steps, *refs),
-        (w, a, b_t),
-        [IN_HBM, ANYWHERE, ANYWHERE],
+        (w, a) + ((b_t,) if more else ()),
+        [IN_HBM] + [ANYWHERE] * (2 if more else 1),
         [((TALL, width), bf16)],
         [IN_VMEM],
-        [pltpu.VMEM((COLS, LOW), bf16), pltpu.SemaphoreType.DMA((2 * len(steps) + 1,))],
+        ([pltpu.VMEM((COLS, LOW), bf16)] if more else [])
+        + [pltpu.SemaphoreType.DMA((2 * len(steps) + 1,))],
         0,
         4 * TALL * width,
         vmem,
@@ -129,9 +132,9 @@
 def part_kernel(n, first, *refs):
     wx, mine, other = refs[0], refs[1 : 1 + n], refs[1 + n : 1 + 2 * n]
     acc, out, xs, sem = (None, *refs[-3:]) if first else refs[-4:]
+    depth = n * CHIP
     for h in start_all(token_pairs([k * CHIP for k in range(n)], mine, other, xs), sem):
         h.wait()
-    depth = n * CHIP
     for j in range(ROWS // NB):
         cols = slice(j * NB, (j + 1) * NB)
         part = jnp.dot(wx[:, :depth], xs[:, cols], preferred_element_type=f32)
@@ -148,7 +151,10 @@
         [IN_VMEM, IN_HBM if first else IN_VMEM] + [IN_VMEM] * (len(args) - 2),
         [((TALL, ROWS), f32)],
         [IN_VMEM],
-        [pltpu.VMEM((n * CHIP, ROWS), bf16), pltpu.SemaphoreType.DMA((2 * n,))],
+        [
+            pltpu.VMEM((n * CHIP, ROWS), bf16),
+            pltpu.SemaphoreType.DMA((2 * n,)),
+        ],
         2 * TALL * n * CHIP * ROWS,
         2 * n * CHIP * (TALL + ROWS),
         14,
@@ -232,29 +238,32 @@
 
 
 def pair_kernel(got, out):
-    out[...] = got[:, WIDE:]
+    there = got[:, WIDE : 2 * WIDE].astype(f32)
+    odd = jnp.full((got.shape[0], SHARD), pair_now(), jnp.int32) == 0
+    out[:, :COLS] = got[:, 2 * WIDE : 2 * WIDE + COLS]
+    out[:, COLS:] = jnp.where(odd, there[:, 64:], there[:, :SHARD]).astype(bf16)
 
 
 def pair_message(got):
-    shape = (got.shape[0], PAY - WIDE)
+    shape = (got.shape[0], COLS + SHARD)
     (out,) = kernel_call(
         pair_kernel, (got,), [IN_VMEM], [(shape, bf16)], [IN_VMEM], [], 0, 4 * math.prod(shape), 4
     )
     return out
 
 
-def update_kernel(got, far, out, wide, up, sem):
-    def outer(left, right):
-        return lax.dot_general(
-            left, right, (((0,), (0,)), ((), ())), preferred_element_type=f32
-        )
-
-    wide[...] = (
-        outer(got[:, :WIDE], got[:, 2 * WIDE : 2 * WIDE + COLS])
-        + outer(far[:, :WIDE], far[:, WIDE : WIDE + COLS])
-    )
+def outer(left, right):
+    return lax.dot_general(left, right, (((0,), (0,)), ((), ())), preferred_element_type=f32)
+
+
+def own_update_kernel(got, out):
+    out[...] = outer(got[:, :WIDE], got[:, 2 * WIDE : 2 * WIDE + COLS])
+
+
+def update_kernel(own, far, out, up, sem):
     first = pl.multiple_of(pair_now() * 64, 64)
-    up[...] = (wide[pl.ds(first, SHARD), :] * (1.0 / math.sqrt(512))).astype(bf16)
+    total = own[pl.ds(first, SHARD), :] + outer(far[:, COLS:], far[:, :COLS])
+    up[...] = (total * (1.0 / math.sqrt(512))).astype(bf16)
     copy = pltpu.make_async_copy(up, out, sem)
     copy.start()
     copy.wait()
@@ -293,9 +302,7 @@
     got = lax.all_to_all(payload, "pop", 0, 0, axis_index_groups=Z_GROUPS, tiled=True)
     got = got.reshape(ZS * LOW, PAY)
 
-    near_w = weights(NEAR, 0, w, a, b_t, 44)
-    far_w = weights(FAR, 128, w, a, b_t, 42)
-
+    near_w = weights(NEAR, 0, w, a, 44)
     two_x = send(low_x, X_UP)
     far_high = send(far_y, X_DOWN)
     far_low = send(low_x, Y_SWAP)
@@ -305,23 +312,39 @@
     two_x, far_high, far_low, acc, got = lax.optimization_barrier(
         (two_x, far_high, far_low, acc, got)
     )
+    message, far_low, far_high = lax.optimization_barrier(
+        (pair_message(got), far_low, far_high)
+    )
     e = [send(far_low[: SHARD // 2], X_UP), send(far_high[SHARD // 2 :], X_DOWN)]
     o2 = [swap(two_x), swap(far_high), swap(far_low)]
-    far = lax.ppermute(pair_message(got), "pop", PAIR_SWAP)
+    far = lax.ppermute(message, "pop", PAIR_SWAP)
+    o2[0], b_t = lax.optimization_barrier((o2[0], b_t))
+    far_w = weights(FAR, 128, w, a, 42, b_t)
     acc = part_product(far_w, [two_x, far_high, far_low], o2, acc)
 
-    *e, acc = lax.optimization_barrier((*e, acc))
+    *e, acc, got = lax.optimization_barrier((*e, acc, got))
     oe = [swap(v) for v in e]
+    (own,) = kernel_call(
+        own_update_kernel,
+        (got,),
+        [IN_VMEM],
+        [((WIDE, COLS), f32)],
+        [IN_VMEM],
+        [],
+        2 * 256 * WIDE * COLS,
+        2 * 256 * PAY,
+        6,
+    )
+    acc, own = lax.optimization_barrier((acc, own))
     act = last_product((0, SHARD // 2), far_w, e, oe, acc, member_of_row.reshape(1, ROWS))
     act, far = lax.optimization_barrier((act, far))
     (update,) = kernel_call(
         update_kernel,
-        (got, far),
+        (own, far),
         [IN_VMEM] * 2,
         [((SHARD, COLS), bf16)],
         [IN_HBM],
         [
-            pltpu.VMEM((WIDE, COLS), f32),
             pltpu.VMEM((SHARD, COLS), bf16),
             pltpu.SemaphoreType.DMA,
         ],

time: 73.9 us -> 70.2 us (0.950)
  waiting for transfers between devices: 9.26 us -> 4.71 us
    ppermute x1, waiting for transfers between devices: 4.01 us -> 0.01 us  [body(): far = lax.ppermute(message, 'pop', PAIR_SWAP)]
    ppermute x17, waiting for transfers between devices: 2.67 us -> 1.19 us  [body(): send = lambda v, perm: lax.ppermute(v, 'tp', perm)]
    slice x2, local copies, waits for them, and re-layouts: 0.05 us -> 1.5 us  [body(): e = [send(far_low[:SHARD // 2], X_UP), send(far_high[SHARD // 2:], X_DOWN)]]
    all_to_all x1, waiting for transfers between devices: 2.58 us -> 3.52 us  [body(): lax.all_to_all(payload, 'pop', 0, 0, axis_index_groups=Z_GROUPS, tiled=True)]
    unnamed x16, local copies, waits for them, and re-layouts: 4.02 us -> 3.1 us
    pallas_call x8 -> x9, Pallas kernels: 30.7 us -> 30.5 us  [kernel_call(): pl.pallas_call(kernel, out_shape=[jax.ShapeDtypeStruct(shape, dtype) for...]
  transfers between devices with their start and end apart: 19 -> 19, of which waited for: 5 -> 3; matrix products, arithmetic and copies ran while one was open for 0% -> 2% of each run, Pallas kernels for 39% -> 42%
where the time goes in v3:
time: 70.2 us; the launch traced here: 69.9 us
  Pallas kernels  30.5 us (43%)
  starting transfers between devices  29.1 us (41%)
  waiting for transfers between devices  4.71 us (7%)
  local copies, waits for them, and re-layouts  4.6 us (7%)
  between operations  0.99 us (1%)
    pallas_call x9, Pallas kernels, kernel_call(): pl.pallas_call(kernel, out_shape=[jax.ShapeDtypeStruct(shape, dtype) for...  30.5 us
    ppermute x17, starting transfers between devices, body(): send = lambda v, perm: lax.ppermute(v, 'tp', perm)  20.5 us
    all_to_all x1, starting transfers between devices, body(): lax.all_to_all(payload, 'pop', 0, 0, axis_index_groups=Z_GROUPS, tiled=True)  8.2 us
    all_to_all x1, waiting for transfers between devices, body(): lax.all_to_all(payload, 'pop', 0, 0, axis_index_groups=Z_GROUPS, tiled=True)  3.52 us
    unnamed x16, local copies, waits for them, and re-layouts  3.1 us
    slice x2, local copies, waits for them, and re-layouts, body(): e = [send(far_low[:SHARD // 2], X_UP), send(far_high[SHARD // 2:], X_DOWN)]  1.5 us
  transfers between devices with their start and end apart: 19, of which 3 were waited for; matrix products, arithmetic and copies ran while one was open for 2% of the time, Pallas kernels for 42%

profile of v3, /device:TPU:1, one launch (start us, length us, event | category | flops | bytes accessed | tf_op | source)
XLA Modules:
  0.0 69.9 jit_solution(12715650926118956464)
XLA Ops:
  0.6 2.1 %collective-permute-start = (bf16[320,1024]{1,0:T(8,128)(2,1)}, bf16[320,1024]{1,0:T(8,128)(2,1)}, u32[]{:S(2)}, u32[]{:S(2)}) collective-permute-start(bf16[320,1024]{1,0:T(8,128)(2,1)} %bitcast.10), channel_id=1, source_target_pairs={{0,2},{1,3},{2,4},{3,5},{4,6},{5,7},{6,0},{7,1},{8,10},{9,11},{10,... | collective-permute-start | bytes 1966088 | tf_op jit(solution)/shard_map/ppermute | solution.py:276
  2.7 2.9 %collective-permute-start.2 = (bf16[320,1024]{1,0:T(8,128)(2,1)}, bf16[320,1024]{1,0:T(8,128)(2,1)}, u32[]{:S(2)}, u32[]{:S(2)}) collective-permute-start(bf16[320,1024]{1,0:T(8,128)(2,1)} %bitcast.11), channel_id=1, source_target_pairs={{0,8},{1,9},{2,10},{3,11},{4,12},{5,13},{6,14},{7,15},{8,0},{9,1},... | collective-permute-start | bytes 1966088 | tf_op jit(solution)/shard_map/ppermute | solution.py:276
  5.7 1.5 %collective-permute-start.5 = (bf16[320,1024]{1,0:T(8,128)(2,1)}, bf16[320,1024]{1,0:T(8,128)(2,1)}, u32[]{:S(2)}, u32[]{:S(2)}) collective-permute-start(bf16[320,1024]{1,0:T(8,128)(2,1)} %bitcast.12), channel_id=1, source_target_pairs={{0,6},{1,7},{2,0},{3,1},{4,2},{5,3},{6,4},{7,5},{8,14},{9,15},{10,... | collective-permute-start | bytes 1966088 | tf_op jit(solution)/shard_map/ppermute | solution.py:276
  7.1 3.0 %shard_map.77 = (bf16[32,5120]{1,0:T(8,128)(2,1)}, bf16[1088,32]{1,0:T(8,128)(2,1)}, bf16[8,32,1920]{2,1,0:T(8,128)(2,1)}) custom-call(s32[8]{0:T(128)} %rank.1, bf16[8,4,5120]{2,1,0:T(4,128)(2,1)} %a_hbm.1, bf16[8,4,1088]{2,1,0:T(4,128)(2,1)} %b_hbm.1), custom_call_target="tpu_custom_call" | custom-call | bytes 1380352 | tf_op jit(solution)/shard_map/pallas_call | solution.py:51
  10.2 8.2 %all-to-all-start = ((bf16[8,32,1920]{2,1,0:T(8,128)(2,1)}), bf16[8,32,1920]{2,1,0:T(8,128)(2,1)S(1)}, u32[]{:S(2)}, u32[]{:S(2)}) async-start(bf16[8,32,1920]{2,1,0:T(8,128)(2,1)} %get-tuple-element.24), calls=%async_computation | async-start | bytes 1966080 | tf_op jit(solution)/shard_map/all_to_all | solution.py:302
  18.4 1.8 %collective-permute-start.6 = (bf16[320,1024]{1,0:T(8,128)(2,1)}, bf16[320,1024]{1,0:T(8,128)(2,1)S(1)}, u32[]{:S(2)}, u32[]{:S(2)}) collective-permute-start(bf16[320,1024]{1,0:T(8,128)(2,1)} %bitcast.13), channel_id=1, source_target_pairs={{0,1},{1,0},{2,3},{3,2},{4,5},{5,4},{6,7},{7,6},{8,9},{9,8},{10,11... | collective-permute-start | bytes 1966088 | tf_op jit(solution)/shard_map/ppermute | solution.py:276
  20.2 0.0 collective-permute-done.refs_2_
  20.2 0.1 collective-permute-start.7
  20.3 0.0 collective-permute-done.2.refs_4_
  20.3 1.5 %collective-permute-start.9 = (bf16[320,1024]{1,0:T(8,128)(2,1)}, bf16[320,1024]{1,0:T(8,128)(2,1)S(1)}, u32[]{:S(2)}, u32[]{:S(2)}) collective-permute-start(bf16[320,1024]{1,0:T(8,128)(2,1)} %collective-permute-done.2.refs_4_), channel_id=1, source_target_pairs={{0,1},{1,0},{2,3},{3,2},{4,5},{5,4},{6,7},{7,6},{8,9},{9,8},{10,11... | collective-permute-start | bytes 1966088 | tf_op jit(solution)/shard_map/ppermute | solution.py:276
  21.7 0.0 collective-permute-done.5.refs_3_
  21.7 1.4 %collective-permute-start.8 = (bf16[320,1024]{1,0:T(8,128)(2,1)}, bf16[320,1024]{1,0:T(8,128)(2,1)S(1)}, u32[]{:S(2)}, u32[]{:S(2)}) collective-permute-start(bf16[320,1024]{1,0:T(8,128)(2,1)} %collective-permute-done.5.refs_3_), channel_id=1, source_target_pairs={{0,1},{1,0},{2,3},{3,2},{4,5},{5,4},{6,7},{7,6},{8,9},{9,8},{10,11... | collective-permute-start | bytes 1966088 | tf_op jit(solution)/shard_map/ppermute | solution.py:276
  23.1 1.2 %collective-permute-start.1 = (bf16[320,1024]{1,0:T(8,128)(2,1)}, bf16[320,1024]{1,0:T(8,128)(2,1)S(1)}, u32[]{:S(2)}, u32[]{:S(2)}) collective-permute-start(bf16[320,1024]{1,0:T(8,128)(2,1)} %collective-permute-done.refs_2_), channel_id=1, source_target_pairs={{0,2},{1,3},{2,4},{3,5},{4,6},{5,7},{6,0},{7,1},{8,10},{9,11},{10,... | collective-permute-start | bytes 1966088 | tf_op jit(solution)/shard_map/ppermute | solution.py:276
  24.3 0.0 collective-permute-done.6.refs_5_
  24.3 1.5 %collective-permute-start.4 = (bf16[320,1024]{1,0:T(8,128)(2,1)}, bf16[320,1024]{1,0:T(8,128)(2,1)S(1)}, u32[]{:S(2)}, u32[]{:S(2)}) collective-permute-start(bf16[320,1024]{1,0:T(8,128)(2,1)} %collective-permute-done.refs_2_), channel_id=1, source_target_pairs={{0,8},{1,9},{2,10},{3,11},{4,12},{5,13},{6,14},{7,15},{8,0},{9,1},... | collective-permute-start | bytes 1966088 | tf_op jit(solution)/shard_map/ppermute | solution.py:276
  25.9 0.0 collective-permute-done.7.refs_6_
  25.9 1.5 %collective-permute-start.3 = (bf16[320,1024]{1,0:T(8,128)(2,1)}, bf16[320,1024]{1,0:T(8,128)(2,1)S(1)}, u32[]{:S(2)}, u32[]{:S(2)}) collective-permute-start(bf16[320,1024]{1,0:T(8,128)(2,1)} %collective-permute-done.2.refs_4_), channel_id=1, source_target_pairs={{0,6},{1,7},{2,0},{3,1},{4,2},{5,3},{6,4},{7,5},{8,14},{9,15},{10,... | collective-permute-start | bytes 1966088 | tf_op jit(solution)/shard_map/ppermute | solution.py:276
  27.3 1.0 %copy-done.1 = bf16[32,5120]{1,0:T(8,128)(2,1)S(1)} copy-done((bf16[32,5120]{1,0:T(8,128)(2,1)S(1)}, bf16[32,5120]{1,0:T(8,128)(2,1)}, u32[]{:S(2)}) %copy-start.1) | copy-done | bytes 327704
  28.3 2.8 %shard_map.78.refs_0_ = bf16[1120,2560]{1,0:T(8,128)(2,1)S(1)} custom-call(bf16[1088,5120]{1,0:T(8,128)(2,1)} %bitcast.15, bf16[32,5120]{1,0:T(8,128)(2,1)S(1)} %copy-done.1), custom_call_target="tpu_custom_call" | custom-call | bytes 11468800 | tf_op jit(solution)/shard_map/pallas_call | solution.py:51
  31.1 0.0 copy-start.2
  31.1 9.4 %shard_map.79.refs_7_ = f32[1120,1024]{1,0:T(8,128)S(1)} custom-call(bf16[1120,2560]{1,0:T(8,128)(2,1)S(1)} %shard_map.78.refs_0_, bf16[320,1024]{1,0:T(8,128)(2,1)S(1)} %bitcast.14, bf16[320,1024]{1,0:T(8,128)(2,1)} %collective-permute-done.refs_2_, bf16[320,1024]{1,0:T(8,128)(2,1)} %collective-permute-done.5.refs_3_, ...), custom_call_target="tpu_custom_call" | custom-call | flops 5872025600 | bytes 10977280 | tf_op jit(solution)/shard_map/pallas_call | solution.py:51
  40.5 2.1 %copy-done = f32[1120,1024]{1,0:T(8,128)} copy-done((f32[1120,1024]{1,0:T(8,128)}, f32[1120,1024]{1,0:T(8,128)S(1)}, u32[]{:S(2)}) %copy-start) | copy-done | bytes 4587544
  42.6 0.0 collective-permute-done.1.refs_1_
  42.6 0.0 collective-permute-done.4.refs_3_
  42.6 3.5 %all-to-all-done = bf16[8,32,1920]{2,1,0:T(8,128)(2,1)S(1)} async-done(((bf16[8,32,1920]{2,1,0:T(8,128)(2,1)}), bf16[8,32,1920]{2,1,0:T(8,128)(2,1)S(1)}, u32[]{:S(2)}, u32[]{:S(2)}) %all-to-all-start) | async-done | bytes 983072 | tf_op jit(solution)/shard_map/all_to_all | solution.py:302
  46.1 0.5 collective-permute-start.10
  46.6 0.1 shard_map.81
  46.8 0.1 collective-permute-start.13
  46.9 0.5 collective-permute-start.14
  47.4 0.7 %slice.6 = bf16[160,1024]{1,0:T(8,128)(2,1)} slice(bf16[320,1024]{1,0:T(8,128)(2,1)S(1)} %collective-permute-done.4.refs_3_), slice={[0:160], [0:1024]} | slice | bytes 655360 | tf_op jit(solution)/shard_map/slice | solution.py:318
  48.1 0.8 %slice.7 = bf16[160,1024]{1,0:T(8,128)(2,1)} slice(bf16[320,1024]{1,0:T(8,128)(2,1)S(1)} %collective-permute-done.3.refs_2_), slice={[160:320], [0:1024]} | slice | bytes 655360 | tf_op jit(solution)/shard_map/slice | solution.py:318
  48.9 0.0 collective-permute-start.11
  48.9 2.7 %collective-permute-start.12 = (bf16[160,1024]{1,0:T(8,128)(2,1)}, bf16[160,1024]{1,0:T(8,128)(2,1)S(1)}, u32[]{:S(2)}, u32[]{:S(2)}) collective-permute-start(bf16[160,1024]{1,0:T(8,128)(2,1)} %slice.7), channel_id=1, source_target_pairs={{0,6},{1,7},{2,0},{3,1},{4,2},{5,3},{6,4},{7,5},{8,14},{9,15},{10,... | collective-permute-start | bytes 983048 | tf_op jit(solution)/shard_map/ppermute | solution.py:276
  51.6 0.0 collective-permute-done.10.refs_4_
  51.6 0.4 collective-permute-start.17
  52.0 2.8 %shard_map.80.refs_0_ = bf16[1120,2688]{1,0:T(8,128)(2,1)S(1)} custom-call(bf16[1088,5120]{1,0:T(8,128)(2,1)} %bitcast.16, bf16[32,5120]{1,0:T(8,128)(2,1)S(1)} %copy-done.2, bf16[1088,32]{1,0:T(8,128)(2,1)S(1)} %copy-done.3), custom_call_target="tpu_custom_call" | custom-call | bytes 12042240 | tf_op jit(solution)/shard_map/pallas_call | solution.py:51
  54.8 0.0 copy-start.4
  54.8 0.0 collective-permute-done.13.refs_5_
  54.8 6.3 %shard_map.82.refs_5_ = f32[1120,1024]{1,0:T(8,128)S(1)} custom-call(bf16[1120,2688]{1,0:T(8,128)(2,1)S(1)} %shard_map.80.refs_0_, bf16[320,1024]{1,0:T(8,128)(2,1)S(1)} %collective-permute-done.1.refs_1_, bf16[320,1024]{1,0:T(8,128)(2,1)S(1)} %collective-permute-done.3.refs_2_, bf16[320,1024]{1,0:T(8,128)(2,1)S(1)} %collective-permute-done.4.refs_3_, ...), custom_call_target="tpu_custom_call" | custom-call | flops 4404019200 | bytes 8232960 | tf_op jit(solution)/shard_map/pallas_call | solution.py:51
  61.2 0.0 collective-permute-done.11.refs_1_
  61.2 1.2 %collective-permute-start.15 = (bf16[160,1024]{1,0:T(8,128)(2,1)S(1)}, bf16[160,1024]{1,0:T(8,128)(2,1)S(1)}, u32[]{:S(2)}, u32[]{:S(2)}) collective-permute-start(bf16[160,1024]{1,0:T(8,128)(2,1)S(1)} %collective-permute-done.11.refs_1_), channel_id=1, source_target_pairs={{0,1},{1,0},{2,3},{3,2},{4,5},{5,4},{6,7},{7,6},{8,9},{9,8},{10,11... | collective-permute-start | bytes 983048 | tf_op jit(solution)/shard_map/ppermute | solution.py:276
  62.4 0.1 collective-permute-start.16
  62.5 0.5 shard_map.83.own
  63.0 0.7 collective-permute-done.15.refs_3_
  63.7 0.5 collective-permute-done.16.refs_4_
  64.1 4.2 %shard_map.84 = bf16[1088,1024]{1,0:T(8,128)(2,1)} custom-call(bf16[1120,2688]{1,0:T(8,128)(2,1)S(1)} %shard_map.80.refs_0_, bf16[160,1024]{1,0:T(8,128)(2,1)S(1)} %collective-permute-done.11.refs_1_, bf16[160,1024]{1,0:T(8,128)(2,1)S(1)} %collective-permute-done.12.refs_2_, bf16[160,1024]{1,0:T(8,128)(2,1)S(1)} %collective-permute-done.15.refs_3_, ...), custom_call_target="tpu_custom_call" | custom-call | flops 1468006400 | bytes 2744320 | tf_op jit(solution)/shard_map/pallas_call | solution.py:51
  68.4 0.0 collective-permute-done.17.far
  68.4 1.4 %shard_map.85 = bf16[320,1088]{1,0:T(8,128)(2,1)} custom-call(f32[384,1088]{1,0:T(8,128)S(1)} %shard_map.83.own, bf16[256,1408]{1,0:T(8,128)(2,1)S(1)} %collective-permute-done.17.far), custom_call_target="tpu_custom_call" | custom-call | flops 427819008 | bytes 1966080 | tf_op jit(solution)/shard_map/pallas_call | solution.py:51
  (18 shorter events, 0.0 us)
Async XLA Ops:
  0.6 19.5 %collective-permute-start = (bf16[320,1024]{1,0:T(8,128)(2,1)}, bf16[320,1024]{1,0:T(8,128)(2,1)}, u32[]{:S(2)}, u32[]{:S(2)}) collective-permute-start(bf16[320,1024]{1,0:T(8,128)(2,1)} %bitcast.10), channel_id=1, source_target_pairs={{0,2},{1,3},{2,4},{3,5},{4,6},{5,7},{6,0},{7,1},{8,10},{9,11},{10,... | collective-permute-start | bytes 1966088 | tf_op jit(solution)/shard_map/ppermute | solution.py:276
  2.7 17.5 %collective-permute-start.2 = (bf16[320,1024]{1,0:T(8,128)(2,1)}, bf16[320,1024]{1,0:T(8,128)(2,1)}, u32[]{:S(2)}, u32[]{:S(2)}) collective-permute-start(bf16[320,1024]{1,0:T(8,128)(2,1)} %bitcast.11), channel_id=1, source_target_pairs={{0,8},{1,9},{2,10},{3,11},{4,12},{5,13},{6,14},{7,15},{8,0},{9,1},... | collective-permute-start | bytes 1966088 | tf_op jit(solution)/shard_map/ppermute | solution.py:276
  5.7 16.1 %collective-permute-start.5 = (bf16[320,1024]{1,0:T(8,128)(2,1)}, bf16[320,1024]{1,0:T(8,128)(2,1)}, u32[]{:S(2)}, u32[]{:S(2)}) collective-permute-start(bf16[320,1024]{1,0:T(8,128)(2,1)} %bitcast.12), channel_id=1, source_target_pairs={{0,6},{1,7},{2,0},{3,1},{4,2},{5,3},{6,4},{7,5},{8,14},{9,15},{10,... | collective-permute-start | bytes 1966088 | tf_op jit(solution)/shard_map/ppermute | solution.py:276
  10.2 36.0 %all-to-all-start = ((bf16[8,32,1920]{2,1,0:T(8,128)(2,1)}), bf16[8,32,1920]{2,1,0:T(8,128)(2,1)S(1)}, u32[]{:S(2)}, u32[]{:S(2)}) async-start(bf16[8,32,1920]{2,1,0:T(8,128)(2,1)} %get-tuple-element.24), calls=%async_computation | async-start | bytes 1966080 | tf_op jit(solution)/shard_map/all_to_all | solution.py:302
  18.4 6.0 %collective-permute-start.6 = (bf16[320,1024]{1,0:T(8,128)(2,1)}, bf16[320,1024]{1,0:T(8,128)(2,1)S(1)}, u32[]{:S(2)}, u32[]{:S(2)}) collective-permute-start(bf16[320,1024]{1,0:T(8,128)(2,1)} %bitcast.13), channel_id=1, source_target_pairs={{0,1},{1,0},{2,3},{3,2},{4,5},{5,4},{6,7},{7,6},{8,9},{9,8},{10,11... | collective-permute-start | bytes 1966088 | tf_op jit(solution)/shard_map/ppermute | solution.py:276
  20.2 5.7 %collective-permute-start.7 = (bf16[320,1024]{1,0:T(8,128)(2,1)}, bf16[320,1024]{1,0:T(8,128)(2,1)S(1)}, u32[]{:S(2)}, u32[]{:S(2)}) collective-permute-start(bf16[320,1024]{1,0:T(8,128)(2,1)} %collective-permute-done.refs_2_), channel_id=1, source_target_pairs={{0,1},{1,0},{2,3},{3,2},{4,5},{5,4},{6,7},{7,6},{8,9},{9,8},{10,11... | collective-permute-start | bytes 1966088 | tf_op jit(solution)/shard_map/ppermute | solution.py:276
  20.3 10.8 %collective-permute-start.9 = (bf16[320,1024]{1,0:T(8,128)(2,1)}, bf16[320,1024]{1,0:T(8,128)(2,1)S(1)}, u32[]{:S(2)}, u32[]{:S(2)}) collective-permute-start(bf16[320,1024]{1,0:T(8,128)(2,1)} %collective-permute-done.2.refs_4_), channel_id=1, source_target_pairs={{0,1},{1,0},{2,3},{3,2},{4,5},{5,4},{6,7},{7,6},{8,9},{9,8},{10,11... | collective-permute-start | bytes 1966088 | tf_op jit(solution)/shard_map/ppermute | solution.py:276
  21.7 9.4 %collective-permute-start.8 = (bf16[320,1024]{1,0:T(8,128)(2,1)}, bf16[320,1024]{1,0:T(8,128)(2,1)S(1)}, u32[]{:S(2)}, u32[]{:S(2)}) collective-permute-start(bf16[320,1024]{1,0:T(8,128)(2,1)} %collective-permute-done.5.refs_3_), channel_id=1, source_target_pairs={{0,1},{1,0},{2,3},{3,2},{4,5},{5,4},{6,7},{7,6},{8,9},{9,8},{10,11... | collective-permute-start | bytes 1966088 | tf_op jit(solution)/shard_map/ppermute | solution.py:276
  23.1 19.5 %collective-permute-start.1 = (bf16[320,1024]{1,0:T(8,128)(2,1)}, bf16[320,1024]{1,0:T(8,128)(2,1)S(1)}, u32[]{:S(2)}, u32[]{:S(2)}) collective-permute-start(bf16[320,1024]{1,0:T(8,128)(2,1)} %collective-permute-done.refs_2_), channel_id=1, source_target_pairs={{0,2},{1,3},{2,4},{3,5},{4,6},{5,7},{6,0},{7,1},{8,10},{9,11},{10,... | collective-permute-start | bytes 1966088 | tf_op jit(solution)/shard_map/ppermute | solution.py:276
  24.3 18.3 %collective-permute-start.4 = (bf16[320,1024]{1,0:T(8,128)(2,1)}, bf16[320,1024]{1,0:T(8,128)(2,1)S(1)}, u32[]{:S(2)}, u32[]{:S(2)}) collective-permute-start(bf16[320,1024]{1,0:T(8,128)(2,1)} %collective-permute-done.refs_2_), channel_id=1, source_target_pairs={{0,8},{1,9},{2,10},{3,11},{4,12},{5,13},{6,14},{7,15},{8,0},{9,1},... | collective-permute-start | bytes 1966088 | tf_op jit(solution)/shard_map/ppermute | solution.py:276
  25.9 16.8 %collective-permute-start.3 = (bf16[320,1024]{1,0:T(8,128)(2,1)}, bf16[320,1024]{1,0:T(8,128)(2,1)S(1)}, u32[]{:S(2)}, u32[]{:S(2)}) collective-permute-start(bf16[320,1024]{1,0:T(8,128)(2,1)} %collective-permute-done.2.refs_4_), channel_id=1, source_target_pairs={{0,6},{1,7},{2,0},{3,1},{4,2},{5,3},{6,4},{7,5},{8,14},{9,15},{10,... | collective-permute-start | bytes 1966088 | tf_op jit(solution)/shard_map/ppermute | solution.py:276
  27.3 1.0 %copy-start.1 = (bf16[32,5120]{1,0:T(8,128)(2,1)S(1)}, bf16[32,5120]{1,0:T(8,128)(2,1)}, u32[]{:S(2)}) copy-start(bf16[32,5120]{1,0:T(8,128)(2,1)} %get-tuple-element.23.refs_1_) | copy-start | bytes 983044
  28.3 2.8 %copy-start.5 = (bf16[1024,320]{0,1:T(8,128)(2,1)S(1)}, bf16[1024,320]{0,1:T(8,128)(2,1)}, u32[]{:S(2)}) copy-start(bf16[1024,320]{0,1:T(8,128)(2,1)} %param.6) | copy-start | bytes 1966084
  31.1 20.9 %copy-start.2 = (bf16[32,5120]{1,0:T(8,128)(2,1)S(1)}, bf16[32,5120]{1,0:T(8,128)(2,1)}, u32[]{:S(2)}) copy-start(bf16[32,5120]{1,0:T(8,128)(2,1)} %get-tuple-element.23.refs_1_) | copy-start | bytes 983044
  31.1 20.9 %copy-start.3 = (bf16[1088,32]{1,0:T(8,128)(2,1)S(1)}, bf16[1088,32]{1,0:T(8,128)(2,1)}, u32[]{:S(2)}) copy-start(bf16[1088,32]{1,0:T(8,128)(2,1)} %get-tuple-element.27.refs_2_) | copy-start | bytes 208900
  40.5 2.1 %copy-start = (f32[1120,1024]{1,0:T(8,128)}, f32[1120,1024]{1,0:T(8,128)S(1)}, u32[]{:S(2)}) copy-start(f32[1120,1024]{1,0:T(8,128)S(1)} %shard_map.79.refs_7_) | copy-start | bytes 13762564
  46.1 5.4 %collective-permute-start.10 = (bf16[320,1024]{1,0:T(8,128)(2,1)S(1)}, bf16[320,1024]{1,0:T(8,128)(2,1)S(1)}, u32[]{:S(2)}, u32[]{:S(2)}) collective-permute-start(bf16[320,1024]{1,0:T(8,128)(2,1)S(1)} %collective-permute-done.1.refs_1_), channel_id=1, source_target_pairs={{0,1},{1,0},{2,3},{3,2},{4,5},{5,4},{6,7},{7,6},{8,9},{9,8},{10,11... | collective-permute-start | bytes 1966088 | tf_op jit(solution)/shard_map/ppermute | solution.py:276
  46.8 8.0 %collective-permute-start.13 = (bf16[320,1024]{1,0:T(8,128)(2,1)S(1)}, bf16[320,1024]{1,0:T(8,128)(2,1)S(1)}, u32[]{:S(2)}, u32[]{:S(2)}) collective-permute-start(bf16[320,1024]{1,0:T(8,128)(2,1)S(1)} %collective-permute-done.3.refs_2_), channel_id=1, source_target_pairs={{0,1},{1,0},{2,3},{3,2},{4,5},{5,4},{6,7},{7,6},{8,9},{9,8},{10,11... | collective-permute-start | bytes 1966088 | tf_op jit(solution)/shard_map/ppermute | solution.py:276
  46.9 7.9 %collective-permute-start.14 = (bf16[320,1024]{1,0:T(8,128)(2,1)S(1)}, bf16[320,1024]{1,0:T(8,128)(2,1)S(1)}, u32[]{:S(2)}, u32[]{:S(2)}) collective-permute-start(bf16[320,1024]{1,0:T(8,128)(2,1)S(1)} %collective-permute-done.4.refs_3_), channel_id=1, source_target_pairs={{0,1},{1,0},{2,3},{3,2},{4,5},{5,4},{6,7},{7,6},{8,9},{9,8},{10,11... | collective-permute-start | bytes 1966088 | tf_op jit(solution)/shard_map/ppermute | solution.py:276
  48.1 6.7 %slice-start = ((s8[4587520]{0:T(1024)(128)(4,1)}), s8[4194304]{0:T(1024)(128)(4,1)S(1)}, s32[]{:S(2)}) async-start(s8[4587520]{0:T(1024)(128)(4,1)} %bitcast.7), calls=%async_computation.1 | async-start | bytes 8388608
  48.9 12.3 %collective-permute-start.11 = (bf16[160,1024]{1,0:T(8,128)(2,1)}, bf16[160,1024]{1,0:T(8,128)(2,1)S(1)}, u32[]{:S(2)}, u32[]{:S(2)}) collective-permute-start(bf16[160,1024]{1,0:T(8,128)(2,1)} %slice.6), channel_id=1, source_target_pairs={{0,2},{1,3},{2,4},{3,5},{4,6},{5,7},{6,0},{7,1},{8,10},{9,11},{10,... | collective-permute-start | bytes 983048 | tf_op jit(solution)/shard_map/ppermute | solution.py:276
  48.9 12.3 %collective-permute-start.12 = (bf16[160,1024]{1,0:T(8,128)(2,1)}, bf16[160,1024]{1,0:T(8,128)(2,1)S(1)}, u32[]{:S(2)}, u32[]{:S(2)}) collective-permute-start(bf16[160,1024]{1,0:T(8,128)(2,1)} %slice.7), channel_id=1, source_target_pairs={{0,6},{1,7},{2,0},{3,1},{4,2},{5,3},{6,4},{7,5},{8,14},{9,15},{10,... | collective-permute-start | bytes 983048 | tf_op jit(solution)/shard_map/ppermute | solution.py:276
  51.6 16.8 %collective-permute-start.17 = (bf16[256,1408]{1,0:T(8,128)(2,1)S(1)}, bf16[256,1408]{1,0:T(8,128)(2,1)S(1)}, u32[]{:S(2)}, u32[]{:S(2)}) collective-permute-start(bf16[256,1408]{1,0:T(8,128)(2,1)S(1)} %shard_map.81), channel_id=1, source_target_pairs={{0,16},{16,0},{32,48},{48,32},{64,80},{80,64},{96,112},{112,96},{1... | collective-permute-start | bytes 2162696 | tf_op jit(solution)/shard_map/ppermute | solution.py:320
  52.0 2.8 %slice-start.1 = ((s8[4587520]{0:T(1024)(128)(4,1)}), s8[393216]{0:T(1024)(128)(4,1)S(1)}, s32[]{:S(2)}) async-start(s8[4587520]{0:T(1024)(128)(4,1)} %bitcast.7), calls=%async_computation.2 | async-start | bytes 786432
  54.8 9.4 %copy-start.4 = (s32[1024]{0:T(1024)S(1)}, s32[1024]{0:T(1024)}, u32[]{:S(2)}) copy-start(s32[1024]{0:T(1024)} %param.10) | copy-start | bytes 12292
  61.2 2.5 %collective-permute-start.15 = (bf16[160,1024]{1,0:T(8,128)(2,1)S(1)}, bf16[160,1024]{1,0:T(8,128)(2,1)S(1)}, u32[]{:S(2)}, u32[]{:S(2)}) collective-permute-start(bf16[160,1024]{1,0:T(8,128)(2,1)S(1)} %collective-permute-done.11.refs_1_), channel_id=1, source_target_pairs={{0,1},{1,0},{2,3},{3,2},{4,5},{5,4},{6,7},{7,6},{8,9},{9,8},{10,11... | collective-permute-start | bytes 983048 | tf_op jit(solution)/shard_map/ppermute | solution.py:276
  62.4 1.7 %collective-permute-start.16 = (bf16[160,1024]{1,0:T(8,128)(2,1)S(1)}, bf16[160,1024]{1,0:T(8,128)(2,1)S(1)}, u32[]{:S(2)}, u32[]{:S(2)}) collective-permute-start(bf16[160,1024]{1,0:T(8,128)(2,1)S(1)} %collective-permute-done.12.refs_2_), channel_id=1, source_target_pairs={{0,1},{1,0},{2,3},{3,2},{4,5},{5,4},{6,7},{7,6},{8,9},{9,8},{10,11... | collective-permute-start | bytes 983048 | tf_op jit(solution)/shard_map/ppermute | solution.py:276

commit v4 on v3

--- a/solution.py
+++ b/solution.py
@@ -237,19 +237,29 @@
         out[z, :, 2 * WIDE :] = scaled
 
 
-def pair_kernel(got, out):
+def pair_kernel(got, low, high, out, low_half, high_half):
+    low_half[...] = low[: SHARD // 2, :]
+    high_half[...] = high[SHARD // 2 :, :]
     there = got[:, WIDE : 2 * WIDE].astype(f32)
     odd = jnp.full((got.shape[0], SHARD), pair_now(), jnp.int32) == 0
     out[:, :COLS] = got[:, 2 * WIDE : 2 * WIDE + COLS]
     out[:, COLS:] = jnp.where(odd, there[:, 64:], there[:, :SHARD]).astype(bf16)
 
 
-def pair_message(got):
+def pair_message(got, low, high):
     shape = (got.shape[0], COLS + SHARD)
-    (out,) = kernel_call(
-        pair_kernel, (got,), [IN_VMEM], [(shape, bf16)], [IN_VMEM], [], 0, 4 * math.prod(shape), 4
-    )
-    return out
+    half = (SHARD // 2, ROWS)
+    return kernel_call(
+        pair_kernel,
+        (got, low, high),
+        [IN_VMEM] * 3,
+        [(shape, bf16), (half, bf16), (half, bf16)],
+        [IN_VMEM] * 3,
+        [],
+        0,
+        4 * math.prod(shape),
+        4,
+    )
 
 
 def outer(left, right):
@@ -312,10 +322,8 @@
     two_x, far_high, far_low, acc, got = lax.optimization_barrier(
         (two_x, far_high, far_low, acc, got)
     )
-    message, far_low, far_high = lax.optimization_barrier(
-        (pair_message(got), far_low, far_high)
-    )
-    e = [send(far_low[: SHARD // 2], X_UP), send(far_high[SHARD // 2 :], X_DOWN)]
+    message, low_half, high_half = pair_message(got, far_low, far_high)
+    e = [send(low_half, X_UP), send(high_half, X_DOWN)]
     o2 = [swap(two_x), swap(far_high), swap(far_low)]
     far = lax.ppermute(message, "pop", PAIR_SWAP)
     o2[0], b_t = lax.optimization_barrier((o2[0], b_t))

time: 70.2 us -> 69 us (0.983)
  local copies, waits for them, and re-layouts: 4.6 us -> 3.09 us
    slice x2 -> x0, local copies, waits for them, and re-layouts: 1.5 us -> none  [body(): e = [send(far_low[:SHARD // 2], X_UP), send(far_high[SHARD // 2:], X_DOWN)]]
  transfers between devices with their start and end apart: 19 -> 19, of which waited for: 3 -> 4; matrix products, arithmetic and copies ran while one was open for 2% -> 0% of each run, Pallas kernels for 42% -> 42%
where the time goes in v4:
time: 69 us; the launch traced here: 68.7 us
  Pallas kernels  30.5 us (44%)
  starting transfers between devices  28.8 us (42%)
  waiting for transfers between devices  5.33 us (8%)
  local copies, waits for them, and re-layouts  3.09 us (4%)
  between operations  0.99 us (1%)
    pallas_call x9, Pallas kernels, kernel_call(): pl.pallas_call(kernel, out_shape=[jax.ShapeDtypeStruct(shape, dtype) for...  30.5 us
    ppermute x17, starting transfers between devices, body(): send = lambda v, perm: lax.ppermute(v, 'tp', perm)  20.2 us
    all_to_all x1, starting transfers between devices, body(): lax.all_to_all(payload, 'pop', 0, 0, axis_index_groups=Z_GROUPS, tiled=True)  8.2 us
    all_to_all x1, waiting for transfers between devices, body(): lax.all_to_all(payload, 'pop', 0, 0, axis_index_groups=Z_GROUPS, tiled=True)  3.52 us
    unnamed x16, local copies, waits for them, and re-layouts  3.09 us
  transfers between devices with their start and end apart: 19, of which 4 were waited for; matrix products, arithmetic and copies ran while one was open for 0% of the time, Pallas kernels for 42%

profile of v4, /device:TPU:1, one launch (start us, length us, event | category | flops | bytes accessed | tf_op | source)
XLA Modules:
  0.0 68.7 jit_solution(5197213910413869533)
XLA Ops:
  0.6 2.1 %collective-permute-start = (bf16[320,1024]{1,0:T(8,128)(2,1)}, bf16[320,1024]{1,0:T(8,128)(2,1)}, u32[]{:S(2)}, u32[]{:S(2)}) collective-permute-start(bf16[320,1024]{1,0:T(8,128)(2,1)} %bitcast.10), channel_id=1, source_target_pairs={{0,2},{1,3},{2,4},{3,5},{4,6},{5,7},{6,0},{7,1},{8,10},{9,11},{10,... | collective-permute-start | bytes 1966088 | tf_op jit(solution)/shard_map/ppermute | solution.py:286
  2.7 2.9 %collective-permute-start.2 = (bf16[320,1024]{1,0:T(8,128)(2,1)}, bf16[320,1024]{1,0:T(8,128)(2,1)}, u32[]{:S(2)}, u32[]{:S(2)}) collective-permute-start(bf16[320,1024]{1,0:T(8,128)(2,1)} %bitcast.11), channel_id=1, source_target_pairs={{0,8},{1,9},{2,10},{3,11},{4,12},{5,13},{6,14},{7,15},{8,0},{9,1},... | collective-permute-start | bytes 1966088 | tf_op jit(solution)/shard_map/ppermute | solution.py:286
  5.7 1.5 %collective-permute-start.5 = (bf16[320,1024]{1,0:T(8,128)(2,1)}, bf16[320,1024]{1,0:T(8,128)(2,1)}, u32[]{:S(2)}, u32[]{:S(2)}) collective-permute-start(bf16[320,1024]{1,0:T(8,128)(2,1)} %bitcast.12), channel_id=1, source_target_pairs={{0,6},{1,7},{2,0},{3,1},{4,2},{5,3},{6,4},{7,5},{8,14},{9,15},{10,... | collective-permute-start | bytes 1966088 | tf_op jit(solution)/shard_map/ppermute | solution.py:286
  7.1 3.0 %shard_map.77 = (bf16[32,5120]{1,0:T(8,128)(2,1)}, bf16[1088,32]{1,0:T(8,128)(2,1)}, bf16[8,32,1920]{2,1,0:T(8,128)(2,1)}) custom-call(s32[8]{0:T(128)} %rank.1, bf16[8,4,5120]{2,1,0:T(4,128)(2,1)} %a_hbm.1, bf16[8,4,1088]{2,1,0:T(4,128)(2,1)} %b_hbm.1), custom_call_target="tpu_custom_call" | custom-call | bytes 1380352 | tf_op jit(solution)/shard_map/pallas_call | solution.py:51
  10.2 8.2 %all-to-all-start = ((bf16[8,32,1920]{2,1,0:T(8,128)(2,1)}), bf16[8,32,1920]{2,1,0:T(8,128)(2,1)S(1)}, u32[]{:S(2)}, u32[]{:S(2)}) async-start(bf16[8,32,1920]{2,1,0:T(8,128)(2,1)} %get-tuple-element.24), calls=%async_computation | async-start | bytes 1966080 | tf_op jit(solution)/shard_map/all_to_all | solution.py:312
  18.4 1.8 %collective-permute-start.6 = (bf16[320,1024]{1,0:T(8,128)(2,1)}, bf16[320,1024]{1,0:T(8,128)(2,1)S(1)}, u32[]{:S(2)}, u32[]{:S(2)}) collective-permute-start(bf16[320,1024]{1,0:T(8,128)(2,1)} %bitcast.13), channel_id=1, source_target_pairs={{0,1},{1,0},{2,3},{3,2},{4,5},{5,4},{6,7},{7,6},{8,9},{9,8},{10,11... | collective-permute-start | bytes 1966088 | tf_op jit(solution)/shard_map/ppermute | solution.py:286
  20.2 0.0 collective-permute-done.refs_2_
  20.2 0.1 collective-permute-start.7
  20.3 0.0 collective-permute-done.2.refs_4_
  20.3 1.5 %collective-permute-start.9 = (bf16[320,1024]{1,0:T(8,128)(2,1)}, bf16[320,1024]{1,0:T(8,128)(2,1)S(1)}, u32[]{:S(2)}, u32[]{:S(2)}) collective-permute-start(bf16[320,1024]{1,0:T(8,128)(2,1)} %collective-permute-done.2.refs_4_), channel_id=1, source_target_pairs={{0,1},{1,0},{2,3},{3,2},{4,5},{5,4},{6,7},{7,6},{8,9},{9,8},{10,11... | collective-permute-start | bytes 1966088 | tf_op jit(solution)/shard_map/ppermute | solution.py:286
  21.7 1.4 %collective-permute-start.8 = (bf16[320,1024]{1,0:T(8,128)(2,1)}, bf16[320,1024]{1,0:T(8,128)(2,1)S(1)}, u32[]{:S(2)}, u32[]{:S(2)}) collective-permute-start(bf16[320,1024]{1,0:T(8,128)(2,1)} %collective-permute-done.5.refs_3_), channel_id=1, source_target_pairs={{0,1},{1,0},{2,3},{3,2},{4,5},{5,4},{6,7},{7,6},{8,9},{9,8},{10,11... | collective-permute-start | bytes 1966088 | tf_op jit(solution)/shard_map/ppermute | solution.py:286
  23.1 1.2 %collective-permute-start.1 = (bf16[320,1024]{1,0:T(8,128)(2,1)}, bf16[320,1024]{1,0:T(8,128)(2,1)S(1)}, u32[]{:S(2)}, u32[]{:S(2)}) collective-permute-start(bf16[320,1024]{1,0:T(8,128)(2,1)} %collective-permute-done.refs_2_), channel_id=1, source_target_pairs={{0,2},{1,3},{2,4},{3,5},{4,6},{5,7},{6,0},{7,1},{8,10},{9,11},{10,... | collective-permute-start | bytes 1966088 | tf_op jit(solution)/shard_map/ppermute | solution.py:286
  24.3 0.0 collective-permute-done.6.refs_5_
  24.3 1.5 %collective-permute-start.4 = (bf16[320,1024]{1,0:T(8,128)(2,1)}, bf16[320,1024]{1,0:T(8,128)(2,1)S(1)}, u32[]{:S(2)}, u32[]{:S(2)}) collective-permute-start(bf16[320,1024]{1,0:T(8,128)(2,1)} %collective-permute-done.refs_2_), channel_id=1, source_target_pairs={{0,8},{1,9},{2,10},{3,11},{4,12},{5,13},{6,14},{7,15},{8,0},{9,1},... | collective-permute-start | bytes 1966088 | tf_op jit(solution)/shard_map/ppermute | solution.py:286
  25.9 1.5 %collective-permute-start.3 = (bf16[320,1024]{1,0:T(8,128)(2,1)}, bf16[320,1024]{1,0:T(8,128)(2,1)S(1)}, u32[]{:S(2)}, u32[]{:S(2)}) collective-permute-start(bf16[320,1024]{1,0:T(8,128)(2,1)} %collective-permute-done.2.refs_4_), channel_id=1, source_target_pairs={{0,6},{1,7},{2,0},{3,1},{4,2},{5,3},{6,4},{7,5},{8,14},{9,15},{10,... | collective-permute-start | bytes 1966088 | tf_op jit(solution)/shard_map/ppermute | solution.py:286
  27.3 1.0 %copy-done.1 = bf16[32,5120]{1,0:T(8,128)(2,1)S(1)} copy-done((bf16[32,5120]{1,0:T(8,128)(2,1)S(1)}, bf16[32,5120]{1,0:T(8,128)(2,1)}, u32[]{:S(2)}) %copy-start.1) | copy-done | bytes 327704
  28.3 2.8 %shard_map.78.refs_0_ = bf16[1120,2560]{1,0:T(8,128)(2,1)S(1)} custom-call(bf16[1088,5120]{1,0:T(8,128)(2,1)} %bitcast.15, bf16[32,5120]{1,0:T(8,128)(2,1)S(1)} %copy-done.1), custom_call_target="tpu_custom_call" | custom-call | bytes 11468800 | tf_op jit(solution)/shard_map/pallas_call | solution.py:51
  31.1 0.0 copy-start.2
  31.1 0.0 collective-permute-done.8.refs_7_
  31.1 9.4 %shard_map.79.refs_7_ = f32[1120,1024]{1,0:T(8,128)S(1)} custom-call(bf16[1120,2560]{1,0:T(8,128)(2,1)S(1)} %shard_map.78.refs_0_, bf16[320,1024]{1,0:T(8,128)(2,1)S(1)} %bitcast.14, bf16[320,1024]{1,0:T(8,128)(2,1)} %collective-permute-done.refs_2_, bf16[320,1024]{1,0:T(8,128)(2,1)} %collective-permute-done.5.refs_3_, ...), custom_call_target="tpu_custom_call" | custom-call | flops 5872025600 | bytes 10977280 | tf_op jit(solution)/shard_map/pallas_call | solution.py:51
  40.5 2.1 %copy-done = f32[1120,1024]{1,0:T(8,128)} copy-done((f32[1120,1024]{1,0:T(8,128)}, f32[1120,1024]{1,0:T(8,128)S(1)}, u32[]{:S(2)}) %copy-start) | copy-done | bytes 4587544
  42.6 0.0 collective-permute-done.1.refs_1_
  42.6 0.0 collective-permute-done.4.low.refs_3_
  42.6 0.0 collective-permute-done.3.high.refs_2_
  42.6 3.5 %all-to-all-done = bf16[8,32,1920]{2,1,0:T(8,128)(2,1)S(1)} async-done(((bf16[8,32,1920]{2,1,0:T(8,128)(2,1)}), bf16[8,32,1920]{2,1,0:T(8,128)(2,1)S(1)}, u32[]{:S(2)}, u32[]{:S(2)}) %all-to-all-start) | async-done | bytes 983072 | tf_op jit(solution)/shard_map/all_to_all | solution.py:312
  46.1 0.5 collective-permute-start.10
  46.6 0.0 collective-permute-start.13
  46.7 0.5 collective-permute-start.14
  47.2 0.1 shard_map.81
  47.3 0.1 collective-permute-start.11
  47.4 2.7 %collective-permute-start.12 = (bf16[160,1024]{1,0:T(8,128)(2,1)S(1)}, bf16[160,1024]{1,0:T(8,128)(2,1)S(1)}, u32[]{:S(2)}, u32[]{:S(2)}) collective-permute-start(bf16[160,1024]{1,0:T(8,128)(2,1)S(1)} %get-tuple-element.32), channel_id=1, source_target_pairs={{0,6},{1,7},{2,0},{3,1},{4,2},{5,3},{6,4},{7,5},{8,14},{9,15},{10,... | collective-permute-start | bytes 983048 | tf_op jit(solution)/shard_map/ppermute | solution.py:286
  50.1 0.0 collective-permute-done.10.refs_4_
  50.1 0.4 collective-permute-start.17
  50.5 2.8 %shard_map.80.refs_0_ = bf16[1120,2688]{1,0:T(8,128)(2,1)S(1)} custom-call(bf16[1088,5120]{1,0:T(8,128)(2,1)} %bitcast.16, bf16[32,5120]{1,0:T(8,128)(2,1)S(1)} %copy-done.2, bf16[1088,32]{1,0:T(8,128)(2,1)S(1)} %copy-done.3), custom_call_target="tpu_custom_call" | custom-call | bytes 12042240 | tf_op jit(solution)/shard_map/pallas_call | solution.py:51
  53.3 0.0 copy-start.4
  53.3 0.0 collective-permute-done.13.refs_5_
  53.3 0.0 collective-permute-done.14.refs_6_
  53.3 6.3 %shard_map.82.refs_5_ = f32[1120,1024]{1,0:T(8,128)S(1)} custom-call(bf16[1120,2688]{1,0:T(8,128)(2,1)S(1)} %shard_map.80.refs_0_, bf16[320,1024]{1,0:T(8,128)(2,1)S(1)} %collective-permute-done.1.refs_1_, bf16[320,1024]{1,0:T(8,128)(2,1)S(1)} %collective-permute-done.3.high.refs_2_, bf16[320,1024]{1,0:T(8,128)(2,1)S(1)} %collective-permute-done.4.low.refs_3_, ...), custom_call_target="tpu_custom_call" | custom-call | flops 4404019200 | bytes 8232960 | tf_op jit(solution)/shard_map/pallas_call | solution.py:51
  59.7 0.0 collective-permute-done.11.refs_1_
  59.7 0.0 collective-permute-done.12.refs_2_
  59.7 0.9 %collective-permute-start.15 = (bf16[160,1024]{1,0:T(8,128)(2,1)S(1)}, bf16[160,1024]{1,0:T(8,128)(2,1)S(1)}, u32[]{:S(2)}, u32[]{:S(2)}) collective-permute-start(bf16[160,1024]{1,0:T(8,128)(2,1)S(1)} %collective-permute-done.11.refs_1_), channel_id=1, source_target_pairs={{0,1},{1,0},{2,3},{3,2},{4,5},{5,4},{6,7},{7,6},{8,9},{9,8},{10,11... | collective-permute-start | bytes 983048 | tf_op jit(solution)/shard_map/ppermute | solution.py:286
  60.6 0.1 collective-permute-start.16
  60.7 0.5 shard_map.83.own
  61.2 0.7 collective-permute-done.15.refs_3_
  61.9 0.5 collective-permute-done.16.refs_4_
  62.4 4.2 %shard_map.84 = bf16[1088,1024]{1,0:T(8,128)(2,1)} custom-call(bf16[1120,2688]{1,0:T(8,128)(2,1)S(1)} %shard_map.80.refs_0_, bf16[160,1024]{1,0:T(8,128)(2,1)S(1)} %collective-permute-done.11.refs_1_, bf16[160,1024]{1,0:T(8,128)(2,1)S(1)} %collective-permute-done.12.refs_2_, bf16[160,1024]{1,0:T(8,128)(2,1)S(1)} %collective-permute-done.15.refs_3_, ...), custom_call_target="tpu_custom_call" | custom-call | flops 1468006400 | bytes 2744320 | tf_op jit(solution)/shard_map/pallas_call | solution.py:51
  66.6 0.6 collective-permute-done.17.far
  67.2 1.4 %shard_map.85 = bf16[320,1088]{1,0:T(8,128)(2,1)} custom-call(f32[384,1088]{1,0:T(8,128)S(1)} %shard_map.83.own, bf16[256,1408]{1,0:T(8,128)(2,1)S(1)} %collective-permute-done.17.far), custom_call_target="tpu_custom_call" | custom-call | flops 427819008 | bytes 1966080 | tf_op jit(solution)/shard_map/pallas_call | solution.py:51
  (16 shorter events, 0.0 us)
Async XLA Ops:
  0.6 19.5 %collective-permute-start = (bf16[320,1024]{1,0:T(8,128)(2,1)}, bf16[320,1024]{1,0:T(8,128)(2,1)}, u32[]{:S(2)}, u32[]{:S(2)}) collective-permute-start(bf16[320,1024]{1,0:T(8,128)(2,1)} %bitcast.10), channel_id=1, source_target_pairs={{0,2},{1,3},{2,4},{3,5},{4,6},{5,7},{6,0},{7,1},{8,10},{9,11},{10,... | collective-permute-start | bytes 1966088 | tf_op jit(solution)/shard_map/ppermute | solution.py:286
  2.7 17.5 %collective-permute-start.2 = (bf16[320,1024]{1,0:T(8,128)(2,1)}, bf16[320,1024]{1,0:T(8,128)(2,1)}, u32[]{:S(2)}, u32[]{:S(2)}) collective-permute-start(bf16[320,1024]{1,0:T(8,128)(2,1)} %bitcast.11), channel_id=1, source_target_pairs={{0,8},{1,9},{2,10},{3,11},{4,12},{5,13},{6,14},{7,15},{8,0},{9,1},... | collective-permute-start | bytes 1966088 | tf_op jit(solution)/shard_map/ppermute | solution.py:286
  5.7 16.1 %collective-permute-start.5 = (bf16[320,1024]{1,0:T(8,128)(2,1)}, bf16[320,1024]{1,0:T(8,128)(2,1)}, u32[]{:S(2)}, u32[]{:S(2)}) collective-permute-start(bf16[320,1024]{1,0:T(8,128)(2,1)} %bitcast.12), channel_id=1, source_target_pairs={{0,6},{1,7},{2,0},{3,1},{4,2},{5,3},{6,4},{7,5},{8,14},{9,15},{10,... | collective-permute-start | bytes 1966088 | tf_op jit(solution)/shard_map/ppermute | solution.py:286
  10.2 36.0 %all-to-all-start = ((bf16[8,32,1920]{2,1,0:T(8,128)(2,1)}), bf16[8,32,1920]{2,1,0:T(8,128)(2,1)S(1)}, u32[]{:S(2)}, u32[]{:S(2)}) async-start(bf16[8,32,1920]{2,1,0:T(8,128)(2,1)} %get-tuple-element.24), calls=%async_computation | async-start | bytes 1966080 | tf_op jit(solution)/shard_map/all_to_all | solution.py:312
  18.4 6.0 %collective-permute-start.6 = (bf16[320,1024]{1,0:T(8,128)(2,1)}, bf16[320,1024]{1,0:T(8,128)(2,1)S(1)}, u32[]{:S(2)}, u32[]{:S(2)}) collective-permute-start(bf16[320,1024]{1,0:T(8,128)(2,1)} %bitcast.13), channel_id=1, source_target_pairs={{0,1},{1,0},{2,3},{3,2},{4,5},{5,4},{6,7},{7,6},{8,9},{9,8},{10,11... | collective-permute-start | bytes 1966088 | tf_op jit(solution)/shard_map/ppermute | solution.py:286
  20.2 5.7 %collective-permute-start.7 = (bf16[320,1024]{1,0:T(8,128)(2,1)}, bf16[320,1024]{1,0:T(8,128)(2,1)S(1)}, u32[]{:S(2)}, u32[]{:S(2)}) collective-permute-start(bf16[320,1024]{1,0:T(8,128)(2,1)} %collective-permute-done.refs_2_), channel_id=1, source_target_pairs={{0,1},{1,0},{2,3},{3,2},{4,5},{5,4},{6,7},{7,6},{8,9},{9,8},{10,11... | collective-permute-start | bytes 1966088 | tf_op jit(solution)/shard_map/ppermute | solution.py:286
  20.3 10.8 %collective-permute-start.9 = (bf16[320,1024]{1,0:T(8,128)(2,1)}, bf16[320,1024]{1,0:T(8,128)(2,1)S(1)}, u32[]{:S(2)}, u32[]{:S(2)}) collective-permute-start(bf16[320,1024]{1,0:T(8,128)(2,1)} %collective-permute-done.2.refs_4_), channel_id=1, source_target_pairs={{0,1},{1,0},{2,3},{3,2},{4,5},{5,4},{6,7},{7,6},{8,9},{9,8},{10,11... | collective-permute-start | bytes 1966088 | tf_op jit(solution)/shard_map/ppermute | solution.py:286
  21.7 9.4 %collective-permute-start.8 = (bf16[320,1024]{1,0:T(8,128)(2,1)}, bf16[320,1024]{1,0:T(8,128)(2,1)S(1)}, u32[]{:S(2)}, u32[]{:S(2)}) collective-permute-start(bf16[320,1024]{1,0:T(8,128)(2,1)} %collective-permute-done.5.refs_3_), channel_id=1, source_target_pairs={{0,1},{1,0},{2,3},{3,2},{4,5},{5,4},{6,7},{7,6},{8,9},{9,8},{10,11... | collective-permute-start | bytes 1966088 | tf_op jit(solution)/shard_map/ppermute | solution.py:286
  23.1 19.5 %collective-permute-start.1 = (bf16[320,1024]{1,0:T(8,128)(2,1)}, bf16[320,1024]{1,0:T(8,128)(2,1)S(1)}, u32[]{:S(2)}, u32[]{:S(2)}) collective-permute-start(bf16[320,1024]{1,0:T(8,128)(2,1)} %collective-permute-done.refs_2_), channel_id=1, source_target_pairs={{0,2},{1,3},{2,4},{3,5},{4,6},{5,7},{6,0},{7,1},{8,10},{9,11},{10,... | collective-permute-start | bytes 1966088 | tf_op jit(solution)/shard_map/ppermute | solution.py:286
  24.3 18.3 %collective-permute-start.4 = (bf16[320,1024]{1,0:T(8,128)(2,1)}, bf16[320,1024]{1,0:T(8,128)(2,1)S(1)}, u32[]{:S(2)}, u32[]{:S(2)}) collective-permute-start(bf16[320,1024]{1,0:T(8,128)(2,1)} %collective-permute-done.refs_2_), channel_id=1, source_target_pairs={{0,8},{1,9},{2,10},{3,11},{4,12},{5,13},{6,14},{7,15},{8,0},{9,1},... | collective-permute-start | bytes 1966088 | tf_op jit(solution)/shard_map/ppermute | solution.py:286
  25.9 16.8 %collective-permute-start.3 = (bf16[320,1024]{1,0:T(8,128)(2,1)}, bf16[320,1024]{1,0:T(8,128)(2,1)S(1)}, u32[]{:S(2)}, u32[]{:S(2)}) collective-permute-start(bf16[320,1024]{1,0:T(8,128)(2,1)} %collective-permute-done.2.refs_4_), channel_id=1, source_target_pairs={{0,6},{1,7},{2,0},{3,1},{4,2},{5,3},{6,4},{7,5},{8,14},{9,15},{10,... | collective-permute-start | bytes 1966088 | tf_op jit(solution)/shard_map/ppermute | solution.py:286
  27.3 1.0 %copy-start.1 = (bf16[32,5120]{1,0:T(8,128)(2,1)S(1)}, bf16[32,5120]{1,0:T(8,128)(2,1)}, u32[]{:S(2)}) copy-start(bf16[32,5120]{1,0:T(8,128)(2,1)} %get-tuple-element.23.refs_1_) | copy-start | bytes 983044
  28.3 2.8 %copy-start.5 = (bf16[1024,320]{0,1:T(8,128)(2,1)S(1)}, bf16[1024,320]{0,1:T(8,128)(2,1)}, u32[]{:S(2)}) copy-start(bf16[1024,320]{0,1:T(8,128)(2,1)} %param.6) | copy-start | bytes 1966084
  31.1 19.4 %copy-start.2 = (bf16[32,5120]{1,0:T(8,128)(2,1)S(1)}, bf16[32,5120]{1,0:T(8,128)(2,1)}, u32[]{:S(2)}) copy-start(bf16[32,5120]{1,0:T(8,128)(2,1)} %get-tuple-element.23.refs_1_) | copy-start | bytes 983044
  31.1 19.4 %copy-start.3 = (bf16[1088,32]{1,0:T(8,128)(2,1)S(1)}, bf16[1088,32]{1,0:T(8,128)(2,1)}, u32[]{:S(2)}) copy-start(bf16[1088,32]{1,0:T(8,128)(2,1)} %get-tuple-element.27.refs_2_) | copy-start | bytes 208900
  40.5 2.1 %copy-start = (f32[1120,1024]{1,0:T(8,128)}, f32[1120,1024]{1,0:T(8,128)S(1)}, u32[]{:S(2)}) copy-start(f32[1120,1024]{1,0:T(8,128)S(1)} %shard_map.79.refs_7_) | copy-start | bytes 13762564
  46.1 3.9 %collective-permute-start.10 = (bf16[320,1024]{1,0:T(8,128)(2,1)S(1)}, bf16[320,1024]{1,0:T(8,128)(2,1)S(1)}, u32[]{:S(2)}, u32[]{:S(2)}) collective-permute-start(bf16[320,1024]{1,0:T(8,128)(2,1)S(1)} %collective-permute-done.1.refs_1_), channel_id=1, source_target_pairs={{0,1},{1,0},{2,3},{3,2},{4,5},{5,4},{6,7},{7,6},{8,9},{9,8},{10,11... | collective-permute-start | bytes 1966088 | tf_op jit(solution)/shard_map/ppermute | solution.py:286
  46.6 6.6 %collective-permute-start.13 = (bf16[320,1024]{1,0:T(8,128)(2,1)S(1)}, bf16[320,1024]{1,0:T(8,128)(2,1)S(1)}, u32[]{:S(2)}, u32[]{:S(2)}) collective-permute-start(bf16[320,1024]{1,0:T(8,128)(2,1)S(1)} %collective-permute-done.3.high.refs_2_), channel_id=1, source_target_pairs={{0,1},{1,0},{2,3},{3,2},{4,5},{5,4},{6,7},{7,6},{8,9},{9,8},{10,11... | collective-permute-start | bytes 1966088 | tf_op jit(solution)/shard_map/ppermute | solution.py:286
  46.7 6.6 %collective-permute-start.14 = (bf16[320,1024]{1,0:T(8,128)(2,1)S(1)}, bf16[320,1024]{1,0:T(8,128)(2,1)S(1)}, u32[]{:S(2)}, u32[]{:S(2)}) collective-permute-start(bf16[320,1024]{1,0:T(8,128)(2,1)S(1)} %collective-permute-done.4.low.refs_3_), channel_id=1, source_target_pairs={{0,1},{1,0},{2,3},{3,2},{4,5},{5,4},{6,7},{7,6},{8,9},{9,8},{10,11... | collective-permute-start | bytes 1966088 | tf_op jit(solution)/shard_map/ppermute | solution.py:286
  47.2 6.1 %slice-start = ((s8[4587520]{0:T(1024)(128)(4,1)}), s8[4194304]{0:T(1024)(128)(4,1)S(1)}, s32[]{:S(2)}) async-start(s8[4587520]{0:T(1024)(128)(4,1)} %bitcast.7), calls=%async_computation.1 | async-start | bytes 8388608
  47.3 12.4 %collective-permute-start.11 = (bf16[160,1024]{1,0:T(8,128)(2,1)S(1)}, bf16[160,1024]{1,0:T(8,128)(2,1)S(1)}, u32[]{:S(2)}, u32[]{:S(2)}) collective-permute-start(bf16[160,1024]{1,0:T(8,128)(2,1)S(1)} %get-tuple-element.31), channel_id=1, source_target_pairs={{0,2},{1,3},{2,4},{3,5},{4,6},{5,7},{6,0},{7,1},{8,10},{9,11},{10,... | collective-permute-start | bytes 983048 | tf_op jit(solution)/shard_map/ppermute | solution.py:286
  47.4 12.3 %collective-permute-start.12 = (bf16[160,1024]{1,0:T(8,128)(2,1)S(1)}, bf16[160,1024]{1,0:T(8,128)(2,1)S(1)}, u32[]{:S(2)}, u32[]{:S(2)}) collective-permute-start(bf16[160,1024]{1,0:T(8,128)(2,1)S(1)} %get-tuple-element.32), channel_id=1, source_target_pairs={{0,6},{1,7},{2,0},{3,1},{4,2},{5,3},{6,4},{7,5},{8,14},{9,15},{10,... | collective-permute-start | bytes 983048 | tf_op jit(solution)/shard_map/ppermute | solution.py:286
  50.1 17.1 %collective-permute-start.17 = (bf16[256,1408]{1,0:T(8,128)(2,1)S(1)}, bf16[256,1408]{1,0:T(8,128)(2,1)S(1)}, u32[]{:S(2)}, u32[]{:S(2)}) collective-permute-start(bf16[256,1408]{1,0:T(8,128)(2,1)S(1)} %get-tuple-element.40), channel_id=1, source_target_pairs={{0,16},{16,0},{32,48},{48,32},{64,80},{80,64},{96,112},{112,96},{1... | collective-permute-start | bytes 2162696 | tf_op jit(solution)/shard_map/ppermute | solution.py:328
  50.5 2.8 %slice-start.1 = ((s8[4587520]{0:T(1024)(128)(4,1)}), s8[393216]{0:T(1024)(128)(4,1)S(1)}, s32[]{:S(2)}) async-start(s8[4587520]{0:T(1024)(128)(4,1)} %bitcast.7), calls=%async_computation.2 | async-start | bytes 786432
  53.3 9.1 %copy-start.4 = (s32[1024]{0:T(1024)S(1)}, s32[1024]{0:T(1024)}, u32[]{:S(2)}) copy-start(s32[1024]{0:T(1024)} %param.10) | copy-start | bytes 12292
  59.7 2.2 %collective-permute-start.15 = (bf16[160,1024]{1,0:T(8,128)(2,1)S(1)}, bf16[160,1024]{1,0:T(8,128)(2,1)S(1)}, u32[]{:S(2)}, u32[]{:S(2)}) collective-permute-start(bf16[160,1024]{1,0:T(8,128)(2,1)S(1)} %collective-permute-done.11.refs_1_), channel_id=1, source_target_pairs={{0,1},{1,0},{2,3},{3,2},{4,5},{5,4},{6,7},{7,6},{8,9},{9,8},{10,11... | collective-permute-start | bytes 983048 | tf_op jit(solution)/shard_map/ppermute | solution.py:286
  60.6 1.7 %collective-permute-start.16 = (bf16[160,1024]{1,0:T(8,128)(2,1)S(1)}, bf16[160,1024]{1,0:T(8,128)(2,1)S(1)}, u32[]{:S(2)}, u32[]{:S(2)}) collective-permute-start(bf16[160,1024]{1,0:T(8,128)(2,1)S(1)} %collective-permute-done.12.refs_2_), channel_id=1, source_target_pairs={{0,1},{1,0},{2,3},{3,2},{4,5},{5,4},{6,7},{7,6},{8,9},{9,8},{10,11... | collective-permute-start | bytes 983048 | tf_op jit(solution)/shard_map/ppermute | solution.py:286
